TPU v7x, 256 devices: a whole 4x4x8 slice. The times are simulated.
256 devices in a mesh: row: 32 (over z, x), col: 8 (over y, core).
Axes of the slice: x: 4, y: 4, z: 8, core: 2. Of those that a mesh axis runs over, the one named last changes fastest.
Arguments:
- panel: float32 [128, 524288], P('col', 'row'), may hold values from -6 to 6
- signs: int32 [524288], P('row'), may hold values from -1 to 1, as said below
- offsets: int32 [32768], P('row'), may hold values from 0 to 16383
- owners: int32 [32768, 1], P('row'), may hold values from 0 to 31; in each aligned block of 1024 rows (0 to 1023, 1024 to 2047, ...) at most 64 rows name the same one
Outputs:
- grams: float32 [32, 128, 128], P('row', 'col')
Inputs may be any that keep to these rules, and one draw needn't show every extreme that they name: `signs`: each entry is +1 or -1. `owners`: in each aligned block of 1024 samples (the list of one source), no owner is named more than 64 times, a bound that some block reaches; every owner is named somewhere.
All inputs are finite; a program needn't handle non-finite values.
Results may differ from a plain program's by a relative error of at most 0.0003.
Values sent between devices are 32-bit elements; how exact they have to be, the bound alone decides.
A program may use at most 128 MiB of HBM per device.

v0:
```python
import jax
import jax.numpy as jnp
from jax import lax
from jax.sharding import PartitionSpec as P


def swapped(x, axis, distance):
    return lax.ppermute(x, axis, [(i, i ^ 1 << distance) for i in range(lax.axis_size(axis))])


def sylvester(order):
    index = jnp.arange(order, dtype=jnp.int32)
    common = jnp.bitwise_and(index[:, None], index[None, :])
    parity = jnp.zeros((order, order), jnp.int32)
    for level in range(max(order.bit_length() - 1, 0)):
        parity = parity + jnp.bitwise_and(jnp.right_shift(common, level), 1)
    return (1 - 2 * (parity % 2)).astype(jnp.float32)


def body(panel, signs, offsets, owners):
    col_width, row_count = panel.shape
    devices = lax.axis_size("row")
    blocks = row_count // 128
    sample_count = offsets.shape[0]
    high = lax.Precision.HIGHEST
    scale = 1.0 / jnp.sqrt(jnp.float32(devices * row_count))
    signed = (panel * signs.astype(jnp.float32)[None, :]).reshape(col_width, 128, blocks)
    inner = jnp.einsum("cab,bd->cad", signed, sylvester(blocks), precision=high)
    mixed = jnp.einsum("ea,cad->ced", sylvester(128), inner, precision=high)
    mixed = mixed.reshape(col_width, row_count) * scale
    my_index = lax.axis_index("row")
    for level in range(devices.bit_length() - 1):
        partner = swapped(mixed, "row", level)
        upper = jnp.bitwise_and(jnp.right_shift(my_index, level), 1) == 1
        mixed = jnp.where(upper, partner - mixed, mixed + partner)
    sampled = jnp.take(mixed, offsets, axis=1)
    full_rows = lax.all_gather(sampled, "col", axis=0, tiled=True)
    total_cols = full_rows.shape[0]
    owner_ids = owners[:, 0]
    capacity = 2 * sample_count // devices
    hits = (owner_ids[:, None] == jnp.arange(devices, dtype=jnp.int32)[None, :]).astype(jnp.int32)
    before = jnp.cumsum(hits, axis=0) - hits
    slot_index = jnp.sum(before * hits, axis=1)
    position = owner_ids * capacity + slot_index
    buffer = jnp.zeros((total_cols, devices * capacity), jnp.float32).at[:, position].set(full_rows)
    received = lax.all_to_all(
        buffer.reshape(total_cols, devices, capacity),
        "row",
        split_axis=1,
        concat_axis=1,
        tiled=True,
    )
    received = received.reshape(total_cols, devices * capacity)
    mine = lax.dynamic_slice_in_dim(received, lax.axis_index("col") * col_width, col_width, 0)
    gram = jnp.einsum("ck,dk->cd", mine, received, precision=high) / sample_count
    return gram[None]


def solution(mesh):
    placed = (P("col", "row"), P("row"), P("row"), P("row", None))
    return jax.shard_map(
        body, mesh=mesh, in_specs=placed, out_specs=P("row", "col", None), check_vma=False
    )
```

profile of v0, /device:TPU:2, one launch (start us, length us, event | category | flops | bytes accessed | tf_op | source)
XLA Modules:
  0.0 333.8 jit_solution(12955752235051832701)
XLA Ops:
  0.0 0.8 convert_element_type.18
  0.8 1.3 multiply_bitcast_fusion
  2.2 0.2 copy.35
  2.4 1.1 fusion.15
  3.5 1.0 fusion
  4.6 0.3 copy.14
  4.9 0.6 copy.39
  5.5 2.4 collective-permute-start
  7.9 4.6 %copy.16 = f32[16,16384]{0,1:T(8,128)} copy(f32[16,16384]{1,0:T(8,128)S(1)} %bitcast.46) | data formatting | bytes 2097152 | tf_op jit(solution)/shard_map/mul | solution.py:30
  12.5 18.0 %collective-permute-done = f32[16,16384]{1,0:T(8,128)S(1)} collective-permute-done((f32[16,16384]{1,0:T(8,128)S(1)}, f32[16,16384]{1,0:T(8,128)S(1)}, u32[]{:S(2)}, u32[]{:S(2)}) %collective-permute-start) | collective-permute-done | bytes 1048608 | tf_op jit(solution)/shard_map/ppermute | solution.py:8
  30.5 4.6 %copy.15 = f32[16,16384]{0,1:T(8,128)} copy(f32[16,16384]{1,0:T(8,128)S(1)} %collective-permute-done) | data formatting | bytes 2097152 | tf_op jit(solution)/shard_map/ppermute | solution.py:8
  35.1 9.8 %add_select_fusion.4 = f32[16,16384]{0,1:T(8,128)} fusion(f32[16,16384]{0,1:T(8,128)} %copy.16, f32[16,16384]{0,1:T(8,128)} %copy.15, pred[]{:T(512)S(6)} %eq.55), kind=kLoop, calls=%fused_computation.6 | loop fusion | flops 786432 | bytes 3145729 | tf_op jit(solution)/shard_map/jit(_where)/select_n | solution.py:35
  44.9 5.1 %copy.19 = f32[16,16384]{1,0:T(8,128)S(1)} copy(f32[16,16384]{0,1:T(8,128)} %add_select_fusion.4) | data formatting | bytes 2097152 | tf_op jit(solution)/shard_map/jit(_where)/select_n | solution.py:35
  50.0 2.2 collective-permute-start.1
  52.2 23.1 %collective-permute-done.1 = f32[16,16384]{1,0:T(8,128)S(1)} collective-permute-done((f32[16,16384]{1,0:T(8,128)S(1)}, f32[16,16384]{1,0:T(8,128)S(1)}, u32[]{:S(2)}, u32[]{:S(2)}) %collective-permute-start.1) | collective-permute-done | bytes 1048608 | tf_op jit(solution)/shard_map/ppermute | solution.py:8
  75.3 4.6 %copy.20 = f32[16,16384]{0,1:T(8,128)} copy(f32[16,16384]{1,0:T(8,128)S(1)} %collective-permute-done.1) | data formatting | bytes 2097152 | tf_op jit(solution)/shard_map/ppermute | solution.py:8
  79.9 9.8 %add_select_fusion.3 = f32[16,16384]{0,1:T(8,128)} fusion(f32[16,16384]{0,1:T(8,128)} %add_select_fusion.4, f32[16,16384]{0,1:T(8,128)} %copy.20, pred[]{:T(512)S(6)} %eq.54), kind=kLoop, calls=%fused_computation.5 | loop fusion | flops 786432 | bytes 3145729 | tf_op jit(solution)/shard_map/jit(_where)/select_n | solution.py:35
  89.7 5.1 %copy.22 = f32[16,16384]{1,0:T(8,128)S(1)} copy(f32[16,16384]{0,1:T(8,128)} %add_select_fusion.3) | data formatting | bytes 2097152 | tf_op jit(solution)/shard_map/jit(_where)/select_n | solution.py:35
  94.8 2.3 collective-permute-start.2
  97.1 21.4 %collective-permute-done.2 = f32[16,16384]{1,0:T(8,128)S(1)} collective-permute-done((f32[16,16384]{1,0:T(8,128)S(1)}, f32[16,16384]{1,0:T(8,128)S(1)}, u32[]{:S(2)}, u32[]{:S(2)}) %collective-permute-start.2) | collective-permute-done | bytes 1048608 | tf_op jit(solution)/shard_map/ppermute | solution.py:8
  118.5 4.6 %copy.23 = f32[16,16384]{0,1:T(8,128)} copy(f32[16,16384]{1,0:T(8,128)S(1)} %collective-permute-done.2) | data formatting | bytes 2097152 | tf_op jit(solution)/shard_map/ppermute | solution.py:8
  123.1 9.8 %add_select_fusion.2 = f32[16,16384]{0,1:T(8,128)} fusion(f32[16,16384]{0,1:T(8,128)} %add_select_fusion.3, f32[16,16384]{0,1:T(8,128)} %copy.23, pred[]{:T(512)S(6)} %eq.53), kind=kLoop, calls=%fused_computation.4 | loop fusion | flops 786432 | bytes 3145729 | tf_op jit(solution)/shard_map/jit(_where)/select_n | solution.py:35
  132.8 5.1 %copy.25 = f32[16,16384]{1,0:T(8,128)S(1)} copy(f32[16,16384]{0,1:T(8,128)} %add_select_fusion.2) | data formatting | bytes 2097152 | tf_op jit(solution)/shard_map/jit(_where)/select_n | solution.py:35
  137.9 3.3 %collective-permute-start.3 = (f32[16,16384]{1,0:T(8,128)S(1)}, f32[16,16384]{1,0:T(8,128)S(1)}, u32[]{:S(2)}, u32[]{:S(2)}) collective-permute-start(f32[16,16384]{1,0:T(8,128)S(1)} %copy.25), channel_id=1, source_target_pairs={{0,64},{8,72},{16,80},{24,88},{32,96},{40,104},{48,112},{56,120},{... | collective-permute-start | bytes 3145736 | tf_op jit(solution)/shard_map/ppermute | solution.py:8
  141.3 43.1 %collective-permute-done.3 = f32[16,16384]{1,0:T(8,128)S(1)} collective-permute-done((f32[16,16384]{1,0:T(8,128)S(1)}, f32[16,16384]{1,0:T(8,128)S(1)}, u32[]{:S(2)}, u32[]{:S(2)}) %collective-permute-start.3) | collective-permute-done | bytes 1048608 | tf_op jit(solution)/shard_map/ppermute | solution.py:8
  184.4 4.6 %copy.26 = f32[16,16384]{0,1:T(8,128)} copy(f32[16,16384]{1,0:T(8,128)S(1)} %collective-permute-done.3) | data formatting | bytes 2097152 | tf_op jit(solution)/shard_map/ppermute | solution.py:8
  189.0 9.8 %add_select_fusion.1 = f32[16,16384]{0,1:T(8,128)} fusion(f32[16,16384]{0,1:T(8,128)} %add_select_fusion.2, f32[16,16384]{0,1:T(8,128)} %copy.26, pred[]{:T(512)S(6)} %eq.52), kind=kLoop, calls=%fused_computation.3 | loop fusion | flops 786432 | bytes 3145729 | tf_op jit(solution)/shard_map/jit(_where)/select_n | solution.py:35
  198.7 0.0 copy-start
  198.7 0.0 copy-start.1
  198.7 5.1 %copy.28 = f32[16,16384]{1,0:T(8,128)S(1)} copy(f32[16,16384]{0,1:T(8,128)} %add_select_fusion.1) | data formatting | bytes 2097152 | tf_op jit(solution)/shard_map/jit(_where)/select_n | solution.py:35
  203.9 6.5 %collective-permute-start.4 = (f32[16,16384]{1,0:T(8,128)S(1)}, f32[16,16384]{1,0:T(8,128)S(1)}, u32[]{:S(2)}, u32[]{:S(2)}) collective-permute-start(f32[16,16384]{1,0:T(8,128)S(1)} %copy.28), channel_id=1, source_target_pairs={{0,128},{8,136},{16,144},{24,152},{32,160},{40,168},{48,176},{56,1... | collective-permute-start | bytes 3145736 | tf_op jit(solution)/shard_map/ppermute | solution.py:8
  210.4 0.0 copy-done
  210.4 9.0 %reduce-window.6 = s32[32,8,128]{2,1,0:T(8,128)S(1)} reduce-window(s32[32,8,128]{2,1,0:T(8,128)S(1)} %fusion.8, s32[]{:T(128)} %constant.29.clone.1), window={size=1x1x128 pad=0_0x0_0x127_0}, to_apply=%region_0.1 | reduce-window | flops 4161536 | bytes 262148 | tf_op jit(solution)/shard_map/reduce-window
  219.4 0.1 slice.10
  219.5 0.1 copy.11
  219.7 0.1 copy.12
  219.8 0.1 broadcast_add_fusion
  219.9 0.0 copy-done.1
  220.0 36.2 %collective-permute-done.4 = f32[16,16384]{1,0:T(8,128)S(1)} collective-permute-done((f32[16,16384]{1,0:T(8,128)S(1)}, f32[16,16384]{1,0:T(8,128)S(1)}, u32[]{:S(2)}, u32[]{:S(2)}) %collective-permute-start.4) | collective-permute-done | bytes 1048608 | tf_op jit(solution)/shard_map/ppermute | solution.py:8
  256.1 4.6 %copy.29 = f32[16,16384]{0,1:T(8,128)} copy(f32[16,16384]{1,0:T(8,128)S(1)} %collective-permute-done.4) | data formatting | bytes 2097152 | tf_op jit(solution)/shard_map/ppermute | solution.py:8
  260.7 9.8 %add_select_fusion = f32[16,16384]{0,1:T(8,128)} fusion(f32[16,16384]{0,1:T(8,128)} %add_select_fusion.1, f32[16,16384]{0,1:T(8,128)} %copy.29, pred[]{:T(512)S(6)} %eq.51), kind=kLoop, calls=%fused_computation.2 | loop fusion | flops 786432 | bytes 3145729 | tf_op jit(solution)/shard_map/jit(_where)/select_n | solution.py:35
  270.5 6.2 %gather_fusion = f32[1024,16]{1,0:T(8,128)S(1)} fusion(f32[16,16384]{0,1:T(8,128)} %add_select_fusion, s32[1024]{0:T(1024)S(1)} %fusion.31), kind=kCustom, calls=%fused_computation | custom fusion | bytes 135168 | tf_op jit(solution)/shard_map/jit(_take)/gather | solution.py:36
  276.7 0.2 select_bitcast_fusion
  276.9 0.2 copy.31
  277.1 13.6 %all_gather.3 = f32[128,1024]{1,0:T(8,128)S(1)} all-gather(f32[16,1024]{1,0:T(8,128)S(1)} %copy.31), channel_id=1, replica_groups=mesh['row'=32,'col'=8] {'col'}, dimensions={0}, use_global_device_ids=true | all-gather | bytes 589824 | tf_op jit(solution)/shard_map/all_gather | solution.py:37
  290.7 0.2 copy.32
  290.8 4.1 %scatter_custom_fusion = f32[128,2048]{0,1:T(8,128)} fusion(s32[1024]{0:T(1024)S(1)} %bitcast.56, f32[1024,128]{1,0:T(8,128)S(1)} %copy.32, f32[]{:T(128)} %constant.24.clone.1), kind=kCustom, calls=%fused_computation.15 | custom fusion | bytes 1048580 | tf_op jit(solution)/shard_map/scatter | solution.py:45
  294.9 7.5 %all-to-all-start = ((f32[128,32,64]{0,2,1:T(8,128)}), f32[128,32,64]{0,2,1:T(8,128)S(1)}, u32[]{:S(2)}, u32[]{:S(2)}) async-start(f32[128,32,64]{0,2,1:T(8,128)} %bitcast.10), calls=%async_computation | async-start | bytes 2097152 | tf_op jit(solution)/shard_map/all_to_all | solution.py:46
  302.5 28.6 %all-to-all-done = f32[128,32,64]{0,2,1:T(8,128)S(1)} async-done(((f32[128,32,64]{0,2,1:T(8,128)}), f32[128,32,64]{0,2,1:T(8,128)S(1)}, u32[]{:S(2)}, u32[]{:S(2)}) %all-to-all-start) | async-done | bytes 1048608 | tf_op jit(solution)/shard_map/all_to_all | solution.py:46
  331.0 2.8 fusion.1
  (7 shorter events, 0.1 us)
Async XLA Ops:
  5.5 25.0 %collective-permute-start = (f32[16,16384]{1,0:T(8,128)S(1)}, f32[16,16384]{1,0:T(8,128)S(1)}, u32[]{:S(2)}, u32[]{:S(2)}) collective-permute-start(f32[16,16384]{1,0:T(8,128)S(1)} %bitcast.45), channel_id=1, source_target_pairs={{0,8},{8,0},{16,24},{24,16},{32,40},{40,32},{48,56},{56,48},{64,72... | collective-permute-start | bytes 3145736 | tf_op jit(solution)/shard_map/ppermute | solution.py:8
  50.0 25.3 %collective-permute-start.1 = (f32[16,16384]{1,0:T(8,128)S(1)}, f32[16,16384]{1,0:T(8,128)S(1)}, u32[]{:S(2)}, u32[]{:S(2)}) collective-permute-start(f32[16,16384]{1,0:T(8,128)S(1)} %copy.19), channel_id=1, source_target_pairs={{0,16},{8,24},{16,0},{24,8},{32,48},{40,56},{48,32},{56,40},{64,80... | collective-permute-start | bytes 3145736 | tf_op jit(solution)/shard_map/ppermute | solution.py:8
  94.8 23.7 %collective-permute-start.2 = (f32[16,16384]{1,0:T(8,128)S(1)}, f32[16,16384]{1,0:T(8,128)S(1)}, u32[]{:S(2)}, u32[]{:S(2)}) collective-permute-start(f32[16,16384]{1,0:T(8,128)S(1)} %copy.22), channel_id=1, source_target_pairs={{0,32},{8,40},{16,48},{24,56},{32,0},{40,8},{48,16},{56,24},{64,96... | collective-permute-start | bytes 3145736 | tf_op jit(solution)/shard_map/ppermute | solution.py:8
  137.9 46.4 %collective-permute-start.3 = (f32[16,16384]{1,0:T(8,128)S(1)}, f32[16,16384]{1,0:T(8,128)S(1)}, u32[]{:S(2)}, u32[]{:S(2)}) collective-permute-start(f32[16,16384]{1,0:T(8,128)S(1)} %copy.25), channel_id=1, source_target_pairs={{0,64},{8,72},{16,80},{24,88},{32,96},{40,104},{48,112},{56,120},{... | collective-permute-start | bytes 3145736 | tf_op jit(solution)/shard_map/ppermute | solution.py:8
  198.7 11.6 %copy-start = (s32[1024,1]{0,1:T(1,128)S(1)}, s32[1024,1]{0,1:T(1,128)}, u32[]{:S(2)}) copy-start(s32[1024,1]{0,1:T(1,128)} %param.7) | copy-start | bytes 12292
  198.7 21.2 %copy-start.1 = (s32[1024]{0:T(1024)S(1)}, s32[1024]{0:T(1024)}, u32[]{:S(2)}) copy-start(s32[1024]{0:T(1024)} %param.6) | copy-start | bytes 12292
  203.9 52.3 %collective-permute-start.4 = (f32[16,16384]{1,0:T(8,128)S(1)}, f32[16,16384]{1,0:T(8,128)S(1)}, u32[]{:S(2)}, u32[]{:S(2)}) collective-permute-start(f32[16,16384]{1,0:T(8,128)S(1)} %copy.28), channel_id=1, source_target_pairs={{0,128},{8,136},{16,144},{24,152},{32,160},{40,168},{48,176},{56,1... | collective-permute-start | bytes 3145736 | tf_op jit(solution)/shard_map/ppermute | solution.py:8
  294.9 36.1 %all-to-all-start = ((f32[128,32,64]{0,2,1:T(8,128)}), f32[128,32,64]{0,2,1:T(8,128)S(1)}, u32[]{:S(2)}, u32[]{:S(2)}) async-start(f32[128,32,64]{0,2,1:T(8,128)} %bitcast.10), calls=%async_computation | async-start | bytes 2097152 | tf_op jit(solution)/shard_map/all_to_all | solution.py:46
where the time goes:
time: 334 us
  waiting for transfers between devices  170 us (51%)
  other arithmetic  60.4 us (18%)
  local copies, waits for them, and re-layouts  60.2 us (18%)
  starting transfers between devices  24.2 us (7%)
  blocking collectives  13.6 us (4%)
  matrix products  4.97 us (1%)
    ppermute x5, waiting for transfers between devices, swapped(): lax.ppermute(x, axis, [(i, i ^ 1 << distance) for i in range(lax.axis_siz...  142 us
    select_n x5, other arithmetic, body(): mixed = jnp.where(upper, partner - mixed, mixed + partner)  48.8 us
    all_to_all x1, waiting for transfers between devices, body(): lax.all_to_all(buffer.reshape(total_cols, devices, capacity), 'row', spli...  28.6 us
    ppermute x5, local copies, waits for them, and re-layouts, swapped(): lax.ppermute(x, axis, [(i, i ^ 1 << distance) for i in range(lax.axis_siz...  23 us
    select_n x4, local copies, waits for them, and re-layouts, body(): mixed = jnp.where(upper, partner - mixed, mixed + partner)  20.5 us
    ppermute x5, starting transfers between devices, swapped(): lax.ppermute(x, axis, [(i, i ^ 1 << distance) for i in range(lax.axis_siz...  16.7 us
    all_gather x1, blocking collectives, body(): full_rows = lax.all_gather(sampled, 'col', axis=0, tiled=True)  13.6 us
    another operation x3, other arithmetic  9.15 us
  transfers between devices with their start and end apart: 6, of which 6 were waited for; matrix products, arithmetic and copies ran while one was open for 4% of the time, Pallas kernels for 0%

commit v1 on v0

v1 whole, which is shorter than its diff:
```python
import functools

import jax
import jax.numpy as jnp
from jax import lax
from jax.experimental import pallas as pl
from jax.experimental.pallas import tpu as pltpu
from jax.sharding import PartitionSpec as P

MESH = pl.DeviceIdType.MESH
F32 = jnp.float32
BF16 = jnp.bfloat16
NT = (((1,), (1,)), ((), ()))
VMEM = pl.BlockSpec(memory_space=pltpu.VMEM)
SLOTS = 32


def place():
    row, col = lax.axis_index("row"), lax.axis_index("col")
    return row // 4, row % 4, col // 2, col % 2


def at(z, x, y, core):
    return {"row": z * 4 + x, "col": y * 2 + core}


def iota(shape, dim):
    return lax.broadcasted_iota(jnp.int32, shape, dim)


def sylvester(order):
    v = iota((order, order), 0) & iota((order, order), 1)
    for shift in (4, 2, 1):
        v = v ^ (v >> shift)
    return (1 - 2 * (v & 1)).astype(F32)


def butterfly(vals):
    vals, step = list(vals), 1
    while step < len(vals):
        for i in range(len(vals)):
            if i & step == 0:
                a, b = vals[i], vals[i + step]
                vals[i], vals[i + step] = a + b, a - b
        step *= 2
    return vals


def split(v):
    hi = v.astype(BF16)
    return hi, (v - hi.astype(F32)).astype(BF16)


def wait_bytes(ref, sem):
    pltpu.make_async_copy(ref, ref, sem).wait()


def mix_kernel(panel, signs, out, y_ref, r_ref, t_ref, send_sem, recv_sem, core_send, core_recv):
    z, x, y, core = place()
    table = sylvester(128).astype(BF16)
    table = jnp.concatenate([table, table], axis=0)

    def inner(i, carry):
        sign = signs[pl.ds(i * 16, 16), :].astype(F32)
        rows = []
        for j in range(16):
            start = pl.multiple_of((i * 16 + j) * 128, 128)
            rows.append(panel[:, pl.ds(start, 128)] * sign[j : j + 1, :])
        hi, lo = split(jnp.concatenate(rows, axis=0))
        pieces = jnp.concatenate([hi, lo], axis=1)
        done = jnp.dot(pieces, table, preferred_element_type=F32)
        y_ref[pl.ds(i * 16, 16)] = done.reshape(16, 16, 128)
        return carry

    lax.fori_loop(0, 8, inner, 0)

    def outer_high(g, carry):
        vals = butterfly([y_ref[g + 8 * j] for j in range(16)])
        for j in range(16):
            y_ref[g + 8 * j] = vals[j]
        return carry

    lax.fori_loop(0, 8, outer_high, 0)

    def outer_low(g, carry):
        vals = butterfly([y_ref[g * 8 + j] for j in range(8)])
        for j in range(8):
            y_ref[g * 8 + j] = vals[j]
        return carry

    lax.fori_loop(0, 16, outer_low, 0)

    slot = y * 32 + z * 4 + x

    def send(i, carry):
        off = (i * 37) % 128
        tz, tx, ty = (z + off // 16) % 8, (x + off // 4 % 4) % 4, (y + off % 4) % 4
        pltpu.make_async_remote_copy(
            src_ref=y_ref.at[tz * 16 + tx * 4 + ty],
            dst_ref=r_ref.at[slot],
            send_sem=send_sem,
            recv_sem=recv_sem,
            device_id=at(tz, tx, ty, core),
            device_id_type=MESH,
        ).start()
        return carry

    lax.fori_loop(1, 128, send, 0)
    r_ref[slot] = y_ref[z * 16 + x * 4 + y]
    wait_bytes(r_ref.at[pl.ds(0, 127)], recv_sem)

    turn = (1 - 2 * core).astype(F32)

    def across(v, carry):
        for h in range(2):
            rows = pl.ds(8 * h, 8)
            low = [r_ref[v * 32 + q, rows, :] for q in range(16)]
            high = [r_ref[v * 32 + 16 + q, rows, :] * turn for q in range(16)]
            kept = butterfly([a + b for a, b in zip(low, high)])
            for p in range(16):
                out[p, v, core, rows, :] = kept[p]
            given = butterfly([a - b for a, b in zip(low, high)])
            for p in range(16):
                t_ref[v, p, rows, :] = given[p]
        pltpu.make_async_remote_copy(
            src_ref=t_ref.at[v],
            dst_ref=out.at[:, v, core],
            send_sem=core_send,
            recv_sem=core_recv,
            device_id=at(z, x, y, 1 - core),
            device_id_type=MESH,
        ).start()
        return carry

    lax.fori_loop(0, 4, across, 0)
    wait_bytes(r_ref.at[pl.ds(0, 127)], send_sem)
    wait_bytes(t_ref, core_send)
    wait_bytes(t_ref, core_recv)


def gram_kernel(mixed, offsets, owners, out, wide, picked):
    z, x, y, core = place()
    slab = z * 16 + x * 4 + y
    for p in range(16):
        hi, lo = split(mixed[p])
        wide[0:128, 128 * p : 128 * p + 128] = hi
        wide[128:256, 128 * p : 128 * p + 128] = lo
    here = offsets[...] - slab * 128
    inside = (here >= 0) & (here < 128)
    mask = jnp.where(inside, 1.0, 0.0).astype(F32)
    before = (iota((128, 128), 0) < iota((128, 128), 1)).astype(F32).astype(BF16)
    rank, seen = [], jnp.zeros((16, 1), F32)
    for b in range(8):
        piece = mask[:, 128 * b : 128 * b + 128]
        rank.append(jnp.dot(piece.astype(BF16), before, preferred_element_type=F32) + seen)
        seen = seen + jnp.sum(piece, axis=1, keepdims=True)
    rank = jnp.where(inside, jnp.concatenate(rank, axis=1), -1.0).astype(jnp.int32)
    lane = jnp.where(inside, here, 0).astype(F32)
    name = jnp.where(inside, owners[...] + 1, 0).astype(F32)
    rounds = (jnp.max(seen).astype(jnp.int32) + SLOTS - 1) // SLOTS
    out[...] = jnp.zeros_like(out)

    def one_round(r, carry):
        names = []
        for g in range(4):
            hot = []
            for p in range(4 * g, 4 * g + 4):
                hot.append(rank[p : p + 1, :] == iota((SLOTS, 1024), 0) + r * SLOTS)
            hot = jnp.concatenate(hot, axis=0).astype(F32).astype(BF16)
            facts = jnp.concatenate([lane[4 * g : 4 * g + 4], name[4 * g : 4 * g + 4]], axis=0)
            found = lax.dot_general(facts.astype(BF16), hot, NT, preferred_element_type=F32)
            which = iota((1, 128), 1) // SLOTS
            at_lane, its_name = jnp.zeros((1, 128), F32), jnp.zeros((1, 128), F32)
            for p in range(4):
                at_lane = jnp.where(which == p, found[p : p + 1, :], at_lane)
                its_name = jnp.where(which == p, found[4 + p : 5 + p, :], its_name)
            spot = jnp.where(its_name > 0.5, at_lane.astype(jnp.int32) + which * 128, -1)
            pick = (iota((512, 128), 0) == spot).astype(F32).astype(BF16)
            got = jnp.dot(wide[:, 512 * g : 512 * g + 512], pick, preferred_element_type=F32)
            picked[:, 128 * g : 128 * g + 128] = got.astype(BF16)
            names.append(its_name)
        names = jnp.concatenate(names, axis=1)

        def one_owner(o, carry):
            member = (names == (o + 1).astype(F32)).astype(F32).astype(BF16)
            both = lax.dot_general(picked[...] * member, picked[...], NT, preferred_element_type=F32)
            total = (both[:128, :128] + both[128:, 128:]) + (both[:128, 128:] + both[128:, :128])
            out[o] += total * (2.0 ** -29)
            return carry

        lax.fori_loop(0, 32, one_owner, 0)
        return carry

    lax.fori_loop(0, rounds, one_round, 0)


def sum_kernel(gram, out, c_ref, ha, hb, a1, b1, sa, sb, a2, b2, sz, zr, s0, r0, s1, r1, s2, r2, s3, r3):
    z, x, y, core = place()

    def push(src, dst, ss, rs, where):
        pltpu.make_async_remote_copy(
            src_ref=src, dst_ref=dst, send_sem=ss, recv_sem=rs, device_id=where, device_id_type=MESH
        ).start()

    push(gram.at[:, :, :, 1 - core], c_ref, s0, r0, at(z, x, y, 1 - core))
    wait_bytes(c_ref, r0)

    def add_core(i, carry):
        for tx in range(4):
            for ty in range(4):
                ha[tx, i, ty] = gram[i, tx, ty, core, 0:8, :] + c_ref[i, tx, ty, 0:8, :]
                hb[ty, i, tx] = gram[i, tx, ty, core, 8:16, :] + c_ref[i, tx, ty, 8:16, :]
        return carry

    lax.fori_loop(0, 8, add_core, 0)
    for d in (2, 1, 3):
        tx, ty = (x + d) % 4, (y + d) % 4
        push(ha.at[tx], a1.at[x], s1.at[0], r1.at[0], at(z, tx, y, core))
        push(hb.at[ty], b1.at[y], s1.at[1], r1.at[1], at(z, x, ty, core))
    a1[x] = ha[x]
    b1[y] = hb[y]
    wait_bytes(a1.at[pl.ds(0, 3)], r1.at[0])
    wait_bytes(b1.at[pl.ds(0, 3)], r1.at[1])

    def add_first(i, carry):
        for t in range(4):
            sa[t, i] = (a1[0, i, t] + a1[1, i, t]) + (a1[2, i, t] + a1[3, i, t])
            sb[t, i] = (b1[0, i, t] + b1[1, i, t]) + (b1[2, i, t] + b1[3, i, t])
        return carry

    lax.fori_loop(0, 8, add_first, 0)
    for d in (2, 1, 3):
        tx, ty = (x + d) % 4, (y + d) % 4
        push(sa.at[ty], a2.at[y], s2.at[0], r2.at[0], at(z, x, ty, core))
        push(sb.at[tx], b2.at[x], s2.at[1], r2.at[1], at(z, tx, y, core))
    a2[y] = sa[y]
    b2[x] = sb[x]
    wait_bytes(a2.at[pl.ds(0, 3)], r2.at[0])
    wait_bytes(b2.at[pl.ds(0, 3)], r2.at[1])
    for i in range(8):
        sz[i, 0:8, :] = (a2[0, i] + a2[1, i]) + (a2[2, i] + a2[3, i])
        sz[i, 8:16, :] = (b2[0, i] + b2[1, i]) + (b2[2, i] + b2[3, i])
    for d in (4, 3, 5, 2, 6, 1, 7):
        tz = (z + d) % 8
        push(sz.at[tz], zr.at[z], s3, r3, at(tz, x, y, core))
    zr[z] = sz[z]
    wait_bytes(zr.at[pl.ds(0, 7)], r3)
    v = [zr[i] for i in range(8)]
    out[...] = ((v[0] + v[1]) + (v[2] + v[3])) + ((v[4] + v[5]) + (v[6] + v[7]))
    wait_bytes(c_ref, s0)
    for n in range(2):
        wait_bytes(a1.at[pl.ds(0, 3)], s1.at[n])
        wait_bytes(a2.at[pl.ds(0, 3)], s2.at[n])
    wait_bytes(zr.at[pl.ds(0, 7)], s3)


def body(panel, signs, offsets, owners):
    params = functools.partial(pltpu.CompilerParams, vmem_limit_bytes=48 << 20)
    dma = pltpu.SemaphoreType.DMA
    listed = lax.all_gather(offsets, "row", axis=0)
    named = lax.all_gather(owners.reshape(-1), "row", axis=0)
    core = lax.axis_index("col") % 2
    listed = lax.dynamic_slice_in_dim(listed, core * 16, 16, 0)
    named = lax.dynamic_slice_in_dim(named, core * 16, 16, 0)
    mixed = pl.pallas_call(
        mix_kernel,
        out_shape=jax.ShapeDtypeStruct((16, 4, 2, 16, 128), F32),
        in_specs=[VMEM] * 2,
        out_specs=VMEM,
        scratch_shapes=[
            pltpu.VMEM((128, 16, 128), F32),
            pltpu.VMEM((128, 16, 128), F32),
            pltpu.VMEM((4, 16, 16, 128), F32),
            dma, dma, dma, dma,
        ],
        compiler_params=params(has_side_effects=True),
        name="mix",
    )(panel, signs.reshape(128, 128))
    gram = pl.pallas_call(
        gram_kernel,
        out_shape=jax.ShapeDtypeStruct((32, 128, 128), F32),
        in_specs=[VMEM] * 3,
        out_specs=VMEM,
        scratch_shapes=[pltpu.VMEM((256, 2048), BF16), pltpu.VMEM((256, 512), BF16)],
        compiler_params=params(),
        name="gram",
    )(mixed.reshape(16, 128, 128), listed, named)
    summed = pl.pallas_call(
        sum_kernel,
        out_shape=jax.ShapeDtypeStruct((16, 128), F32),
        in_specs=[VMEM],
        out_specs=VMEM,
        scratch_shapes=[
            pltpu.VMEM((8, 4, 4, 16, 128), F32),
            pltpu.VMEM((4, 8, 4, 8, 128), F32),
            pltpu.VMEM((4, 8, 4, 8, 128), F32),
            pltpu.VMEM((4, 8, 4, 8, 128), F32),
            pltpu.VMEM((4, 8, 4, 8, 128), F32),
            pltpu.VMEM((4, 8, 8, 128), F32),
            pltpu.VMEM((4, 8, 8, 128), F32),
            pltpu.VMEM((4, 8, 8, 128), F32),
            pltpu.VMEM((4, 8, 8, 128), F32),
            pltpu.VMEM((8, 16, 128), F32),
            pltpu.VMEM((8, 16, 128), F32),
        ] + [dma] * 2 + [dma((2,))] * 4 + [dma] * 2,
        compiler_params=params(has_side_effects=True),
        name="sum",
    )(gram.reshape(8, 4, 4, 2, 16, 128))
    return summed[None]


def solution(mesh):
    placed = (P("col", "row"), P("row"), P("row"), P("row", None))
    return jax.shard_map(
        body, mesh=mesh, in_specs=placed, out_specs=P("row", "col", None), check_vma=False
    )
```

time: 334 us -> 177 us (0.53)
  waiting for transfers between devices: 170 us -> 0 us
  Pallas kernels: 0 us -> 85.1 us
  blocking collectives: 13.6 us -> 86.8 us
  other arithmetic: 60.4 us -> 0.95 us
  local copies, waits for them, and re-layouts: 60.2 us -> 3.26 us
  starting transfers between devices: 24.2 us -> 0 us
  matrix products: 4.97 us -> 0 us
    ppermute x5 -> x0, waiting for transfers between devices: 142 us -> none  [swapped(): lax.ppermute(x, axis, [(i, i ^ 1 << distance) for i in range(lax.axis_siz...]
    pallas_call x0 -> x3, Pallas kernels: none -> 85.1 us  [the longest x1 43.4 us: body(): pl.pallas_call(mix_kernel, out_shape=jax.ShapeDtypeStruct((16, 4, 2, 16,...]
    all_gather x1 -> x2, blocking collectives: 13.6 us -> 86.8 us  [the longest x1 45.8 us: body(): listed = lax.all_gather(offsets, 'row', axis=0)]
    select_n x7 -> x0, other arithmetic: 49 us -> none  [the longest x5 48.8 us: body(): mixed = jnp.where(upper, partner - mixed, mixed + partner)]
    all_to_all x1 -> x0, waiting for transfers between devices: 28.6 us -> none  [body(): lax.all_to_all(buffer.reshape(total_cols, devices, capacity), 'row', spli...]
    ppermute x5 -> x0, local copies, waits for them, and re-layouts: 23 us -> none  [swapped(): lax.ppermute(x, axis, [(i, i ^ 1 << distance) for i in range(lax.axis_siz...]
    select_n x5 -> x0, local copies, waits for them, and re-layouts: 20.6 us -> none  [the longest x4 20.5 us: body(): mixed = jnp.where(upper, partner - mixed, mixed + partner)]
    ppermute x5 -> x0, starting transfers between devices: 16.7 us -> none  [swapped(): lax.ppermute(x, axis, [(i, i ^ 1 << distance) for i in range(lax.axis_siz...]
  transfers between devices with their start and end apart: 6 -> 0, of which waited for: 6 -> 0; matrix products, arithmetic and copies ran while one was open for 4% -> 0% of each run, Pallas kernels for 0% -> 0%
where the time goes in v1:
time: 177 us; the launch traced here: 176 us
  blocking collectives  86.8 us (49%)
  Pallas kernels  85.1 us (48%)
  local copies, waits for them, and re-layouts  3.26 us (2%)
    all_gather x1, blocking collectives, body(): listed = lax.all_gather(offsets, 'row', axis=0)  45.8 us
    pallas_call x1, Pallas kernels, body(): pl.pallas_call(mix_kernel, out_shape=jax.ShapeDtypeStruct((16, 4, 2, 16,...  43.4 us
    all_gather x1, blocking collectives, body(): named = lax.all_gather(owners.reshape(-1), 'row', axis=0)  41 us
    pallas_call x1, Pallas kernels, body(): pl.pallas_call(sum_kernel, out_shape=jax.ShapeDtypeStruct((16, 128), F32)...  30.9 us
    pallas_call x1, Pallas kernels, body(): pl.pallas_call(gram_kernel, out_shape=jax.ShapeDtypeStruct((32, 128, 128)...  10.8 us

profile of v1, /device:TPU:2, one launch (start us, length us, event | category | flops | bytes accessed | tf_op | source)
XLA Modules:
  0.0 176.1 jit_solution(2707579685701262581)
XLA Ops:
  0.0 45.8 %all-gather = s32[32768]{0:T(1024)S(1)} all-gather(s32[1024]{0:T(1024)} %param.6), channel_id=2, replica_groups=mesh['row'=32,'col'=8] {'row'}, dimensions={0}, use_global_device_ids=true | all-gather | bytes 135168 | tf_op jit(solution)/shard_map/all_gather | solution.py:260
  45.9 41.0 %all-gather.1 = s32[32768,1]{0,1:T(1,128)S(1)} all-gather(s32[1024,1]{0,1:T(1,128)} %param.7), channel_id=3, replica_groups=mesh['row'=32,'col'=8] {'row'}, dimensions={0}, use_global_device_ids=true | all-gather | bytes 135168 | tf_op jit(solution)/shard_map/all_gather | solution.py:261
  86.9 0.5 broadcast.4
  87.4 0.9 reduce.3
  88.4 0.0 copy-start
  88.4 1.2 copy-done
  89.6 0.0 copy-start.1
  89.6 0.8 copy-done.1
  90.4 43.4 %mix.1 = f32[16,4,2,16,128]{4,3,2,1,0:T(8,128)S(1)} custom-call(f32[16,16384]{1,0:T(8,128)S(1)} %copy-done, s32[128,128]{1,0:T(8,128)S(1)} %bitcast.7), custom_call_target="tpu_custom_call" | custom-call | tf_op jit(solution)/shard_map/mix/pallas_call | solution.py:265
  133.8 10.8 %gram.1 = f32[32,128,128]{2,1,0:T(8,128)S(1)} custom-call(f32[16,128,128]{2,1,0:T(8,128)S(1)} %bitcast.6, s32[16,1024]{1,0:T(8,128)S(1)} %constant_dynamic-slice_fusion.1.offsets, s32[16,1024]{1,0:T(8,128)S(1)} %constant_dynamic-slice_fusion.owners), custom_call_target="tpu_custom_call" | custom-call | tf_op jit(solution)/shard_map/gram/pallas_call | solution.py:279
  144.6 30.9 %sum.1 = f32[16,128]{1,0:T(8,128)S(1)} custom-call(f32[8,4,4,2,16,128]{5,4,3,2,1,0:T(8,128)S(1)} %bitcast.5), custom_call_target="tpu_custom_call" | custom-call | tf_op jit(solution)/shard_map/sum/pallas_call | solution.py:288
  175.5 0.6 copy.6
  (4 shorter events, 0.1 us)
Async XLA Ops:
  88.4 1.2 copy-start
  89.6 0.8 copy-start.1

commit v2 on v1

--- a/solution.py
+++ b/solution.py
@@ -55,24 +55,60 @@
     pltpu.make_async_copy(ref, ref, sem).wait()
 
 
-def mix_kernel(panel, signs, out, y_ref, r_ref, t_ref, send_sem, recv_sem, core_send, core_recv):
+def greet(z, x, y, core, barrier):
+    for d in range(1, 8):
+        tell(barrier, at((z + d) % 8, x, y, core))
+    for d in range(1, 4):
+        tell(barrier, at(z, (x + d) % 4, y, core))
+        tell(barrier, at(z, x, (y + d) % 4, core))
+    tell(barrier, at(z, x, y, 1 - core))
+
+
+def tell(sem, where):
+    pl.semaphore_signal(sem, inc=1, device_id=where, device_id_type=MESH)
+
+
+def push(src, dst, send_sem, recv_sem, where):
+    pltpu.make_async_remote_copy(
+        src_ref=src, dst_ref=dst, send_sem=send_sem, recv_sem=recv_sem, device_id=where, device_id_type=MESH
+    ).start()
+
+
+def mix_kernel(
+    panel_hbm, signs, offsets, owners, out, lists, panel, y_ref, r_ref, t_ref, mine,
+    load_sem, send_sem, recv_sem, core_send, core_recv, list_send, list_recv, plane_sem, all_sem,
+):
     z, x, y, core = place()
+    barrier = pltpu.get_barrier_semaphore()
+    greet(z, x, y, core, barrier)
+
+    def load(i):
+        span = pl.ds(4096 * i, 4096)
+        return pltpu.make_async_copy(panel_hbm.at[:, span], panel.at[:, span], load_sem.at[i])
+
+    for i in range(4):
+        load(i).start()
+    mine[0:8, :] = offsets[...]
+    mine[8:16, :] = owners[...]
     table = sylvester(128).astype(BF16)
     table = jnp.concatenate([table, table], axis=0)
 
-    def inner(i, carry):
-        sign = signs[pl.ds(i * 16, 16), :].astype(F32)
-        rows = []
-        for j in range(16):
-            start = pl.multiple_of((i * 16 + j) * 128, 128)
-            rows.append(panel[:, pl.ds(start, 128)] * sign[j : j + 1, :])
-        hi, lo = split(jnp.concatenate(rows, axis=0))
-        pieces = jnp.concatenate([hi, lo], axis=1)
-        done = jnp.dot(pieces, table, preferred_element_type=F32)
-        y_ref[pl.ds(i * 16, 16)] = done.reshape(16, 16, 128)
-        return carry
-
-    lax.fori_loop(0, 8, inner, 0)
+    for part in range(4):
+        load(part).wait()
+        for i in range(2 * part, 2 * part + 2):
+            sign = signs[16 * i : 16 * i + 16, :].astype(F32)
+            rows = []
+            for j in range(16):
+                start = (i * 16 + j) * 128
+                rows.append(panel[:, start : start + 128] * sign[j : j + 1, :])
+            hi, lo = split(jnp.concatenate(rows, axis=0))
+            pieces = jnp.concatenate([hi, lo], axis=1)
+            done = jnp.dot(pieces, table, preferred_element_type=F32)
+            y_ref[16 * i : 16 * i + 16] = done.reshape(16, 16, 128)
+
+    pl.semaphore_wait(barrier, 14)
+    for d in range(1, 4):
+        tell(plane_sem, at(z, (x + d) % 4, y, core))
 
     def outer_high(g, carry):
         vals = butterfly([y_ref[g + 8 * j] for j in range(16)])
@@ -81,32 +117,51 @@
         return carry
 
     lax.fori_loop(0, 8, outer_high, 0)
-
-    def outer_low(g, carry):
-        vals = butterfly([y_ref[g * 8 + j] for j in range(8)])
-        for j in range(8):
-            y_ref[g * 8 + j] = vals[j]
-        return carry
-
-    lax.fori_loop(0, 16, outer_low, 0)
+    pl.semaphore_wait(plane_sem, 3)
+    for d in range(1, 4):
+        tell(all_sem, at(z, x, (y + d) % 4, core))
+    pl.semaphore_wait(all_sem, 3)
 
     slot = y * 32 + z * 4 + x
+    to_x = [(x + d) % 4 for d in range(4)]
+    to_y = [(y + d) % 4 for d in range(4)]
+    sends_list = z // 4 == core
 
     def send(i, carry):
-        off = (i * 37) % 128
-        tz, tx, ty = (z + off // 16) % 8, (x + off // 4 % 4) % 4, (y + off % 4) % 4
-        pltpu.make_async_remote_copy(
-            src_ref=y_ref.at[tz * 16 + tx * 4 + ty],
-            dst_ref=r_ref.at[slot],
-            send_sem=send_sem,
-            recv_sem=recv_sem,
-            device_id=at(tz, tx, ty, core),
-            device_id_type=MESH,
-        ).start()
-        return carry
-
-    lax.fori_loop(1, 128, send, 0)
+        tz = (z + i * 3 + 4) % 8
+        for g in range(2):
+            vals = butterfly([y_ref[tz * 16 + g * 8 + j] for j in range(8)])
+            for j in range(8):
+                y_ref[tz * 16 + g * 8 + j] = vals[j]
+        for dx in range(4):
+            for dy in range(4):
+                def go():
+                    push(
+                        y_ref.at[tz * 16 + to_x[dx] * 4 + to_y[dy]], r_ref.at[slot],
+                        send_sem, recv_sem, at(tz, to_x[dx], to_y[dy], core),
+                    )
+                def go_list():
+                    push(mine, lists.at[z % 4 * 4 + x], list_send, list_recv, at(tz, to_x[dx], y, core))
+                if dx or dy:
+                    go()
+                else:
+                    pl.when(tz != z)(go)
+                if dy == 0:
+                    pl.when(sends_list if dx else sends_list & (tz != z))(go_list)
+        return carry
+
+    lax.fori_loop(0, 8, send, 0)
     r_ref[slot] = y_ref[z * 16 + x * 4 + y]
+
+    @pl.when(sends_list)
+    def _():
+        lists[z % 4 * 4 + x] = mine[...]
+        wait_bytes(lists.at[pl.ds(0, 15)], list_recv)
+
+    @pl.when(jnp.logical_not(sends_list))
+    def _():
+        wait_bytes(lists, list_recv)
+
     wait_bytes(r_ref.at[pl.ds(0, 127)], recv_sem)
 
     turn = (1 - 2 * core).astype(F32)
@@ -116,36 +171,36 @@
             rows = pl.ds(8 * h, 8)
             low = [r_ref[v * 32 + q, rows, :] for q in range(16)]
             high = [r_ref[v * 32 + 16 + q, rows, :] * turn for q in range(16)]
+            given = butterfly([a - b for a, b in zip(low, high)])
+            for p in range(16):
+                t_ref[v, p, rows, :] = given[p]
             kept = butterfly([a + b for a, b in zip(low, high)])
             for p in range(16):
                 out[p, v, core, rows, :] = kept[p]
-            given = butterfly([a - b for a, b in zip(low, high)])
-            for p in range(16):
-                t_ref[v, p, rows, :] = given[p]
-        pltpu.make_async_remote_copy(
-            src_ref=t_ref.at[v],
-            dst_ref=out.at[:, v, core],
-            send_sem=core_send,
-            recv_sem=core_recv,
-            device_id=at(z, x, y, 1 - core),
-            device_id_type=MESH,
-        ).start()
+        push(t_ref.at[v], out.at[:, v, core], core_send, core_recv, at(z, x, y, 1 - core))
         return carry
 
     lax.fori_loop(0, 4, across, 0)
     wait_bytes(r_ref.at[pl.ds(0, 127)], send_sem)
+
+    @pl.when(sends_list)
+    def _():
+        for n in range(31):
+            wait_bytes(mine, list_send)
+
     wait_bytes(t_ref, core_send)
     wait_bytes(t_ref, core_recv)
 
 
-def gram_kernel(mixed, offsets, owners, out, wide, picked):
+def gram_kernel(mixed, lists, out, wide, picked):
     z, x, y, core = place()
     slab = z * 16 + x * 4 + y
     for p in range(16):
         hi, lo = split(mixed[p])
         wide[0:128, 128 * p : 128 * p + 128] = hi
         wide[128:256, 128 * p : 128 * p + 128] = lo
-    here = offsets[...] - slab * 128
+    here = jnp.concatenate([lists[:, b, :] for b in range(8)], axis=1) - slab * 128
+    owner = jnp.concatenate([lists[:, 8 + b, :] for b in range(8)], axis=1)
     inside = (here >= 0) & (here < 128)
     mask = jnp.where(inside, 1.0, 0.0).astype(F32)
     before = (iota((128, 128), 0) < iota((128, 128), 1)).astype(F32).astype(BF16)
@@ -156,7 +211,7 @@
         seen = seen + jnp.sum(piece, axis=1, keepdims=True)
     rank = jnp.where(inside, jnp.concatenate(rank, axis=1), -1.0).astype(jnp.int32)
     lane = jnp.where(inside, here, 0).astype(F32)
-    name = jnp.where(inside, owners[...] + 1, 0).astype(F32)
+    name = jnp.where(inside, owner + 1, 0).astype(F32)
     rounds = (jnp.max(seen).astype(jnp.int32) + SLOTS - 1) // SLOTS
     out[...] = jnp.zeros_like(out)
 
@@ -197,11 +252,9 @@
 def sum_kernel(gram, out, c_ref, ha, hb, a1, b1, sa, sb, a2, b2, sz, zr, s0, r0, s1, r1, s2, r2, s3, r3):
     z, x, y, core = place()
 
-    def push(src, dst, ss, rs, where):
-        pltpu.make_async_remote_copy(
-            src_ref=src, dst_ref=dst, send_sem=ss, recv_sem=rs, device_id=where, device_id_type=MESH
-        ).start()
-
+    barrier = pltpu.get_barrier_semaphore()
+    greet(z, x, y, core, barrier)
+    pl.semaphore_wait(barrier, 14)
     push(gram.at[:, :, :, 1 - core], c_ref, s0, r0, at(z, x, y, 1 - core))
     wait_bytes(c_ref, r0)
 
@@ -257,34 +310,35 @@
 def body(panel, signs, offsets, owners):
     params = functools.partial(pltpu.CompilerParams, vmem_limit_bytes=48 << 20)
     dma = pltpu.SemaphoreType.DMA
-    listed = lax.all_gather(offsets, "row", axis=0)
-    named = lax.all_gather(owners.reshape(-1), "row", axis=0)
-    core = lax.axis_index("col") % 2
-    listed = lax.dynamic_slice_in_dim(listed, core * 16, 16, 0)
-    named = lax.dynamic_slice_in_dim(named, core * 16, 16, 0)
-    mixed = pl.pallas_call(
+    mixed, lists = pl.pallas_call(
         mix_kernel,
-        out_shape=jax.ShapeDtypeStruct((16, 4, 2, 16, 128), F32),
-        in_specs=[VMEM] * 2,
-        out_specs=VMEM,
+        out_shape=[
+            jax.ShapeDtypeStruct((16, 4, 2, 16, 128), F32),
+            jax.ShapeDtypeStruct((16, 16, 128), jnp.int32),
+        ],
+        in_specs=[pl.BlockSpec(memory_space=pl.ANY)] + [VMEM] * 3,
+        out_specs=[VMEM] * 2,
         scratch_shapes=[
+            pltpu.VMEM((16, 16384), F32),
             pltpu.VMEM((128, 16, 128), F32),
             pltpu.VMEM((128, 16, 128), F32),
             pltpu.VMEM((4, 16, 16, 128), F32),
-            dma, dma, dma, dma,
+            pltpu.VMEM((16, 128), jnp.int32),
+            dma((4,)), dma, dma, dma, dma, dma, dma,
+            pltpu.SemaphoreType.REGULAR, pltpu.SemaphoreType.REGULAR,
         ],
-        compiler_params=params(has_side_effects=True),
+        compiler_params=params(has_side_effects=True, collective_id=1),
         name="mix",
-    )(panel, signs.reshape(128, 128))
+    )(panel, signs.reshape(128, 128), offsets.reshape(8, 128), owners.reshape(8, 128))
     gram = pl.pallas_call(
         gram_kernel,
         out_shape=jax.ShapeDtypeStruct((32, 128, 128), F32),
-        in_specs=[VMEM] * 3,
+        in_specs=[VMEM] * 2,
         out_specs=VMEM,
         scratch_shapes=[pltpu.VMEM((256, 2048), BF16), pltpu.VMEM((256, 512), BF16)],
         compiler_params=params(),
         name="gram",
-    )(mixed.reshape(16, 128, 128), listed, named)
+    )(mixed.reshape(16, 128, 128), lists)
     summed = pl.pallas_call(
         sum_kernel,
         out_shape=jax.ShapeDtypeStruct((16, 128), F32),
@@ -303,7 +357,7 @@
             pltpu.VMEM((8, 16, 128), F32),
             pltpu.VMEM((8, 16, 128), F32),
         ] + [dma] * 2 + [dma((2,))] * 4 + [dma] * 2,
-        compiler_params=params(has_side_effects=True),
+        compiler_params=params(has_side_effects=True, collective_id=2),
         name="sum",
     )(gram.reshape(8, 4, 4, 2, 16, 128))
     return summed[None]

time: 177 us -> 82.2 us (0.46)
  blocking collectives: 86.8 us -> 0 us
  Pallas kernels: 85.1 us -> 77 us
    all_gather x2 -> x0, blocking collectives: 86.8 us -> none  [the longest x1 45.8 us: body(): listed = lax.all_gather(offsets, 'row', axis=0)]
    pallas_call x1, Pallas kernels: 30.9 us -> 23.5 us  [body(): pl.pallas_call(sum_kernel, out_shape=jax.ShapeDtypeStruct((16, 128), F32)...]
    unnamed x5 -> x9, local copies, waits for them, and re-layouts: 2.66 us -> 4.04 us
where the time goes in v2:
time: 82.2 us; the launch traced here: 81.1 us
  Pallas kernels  77 us (94%)
  local copies, waits for them, and re-layouts  4.04 us (5%)
    pallas_call x1, Pallas kernels, body(): pl.pallas_call(mix_kernel, out_shape=[jax.ShapeDtypeStruct((16, 4, 2, 16,...  42.6 us
    pallas_call x1, Pallas kernels, body(): pl.pallas_call(sum_kernel, out_shape=jax.ShapeDtypeStruct((16, 128), F32)...  23.5 us
    pallas_call x1, Pallas kernels, body(): pl.pallas_call(gram_kernel, out_shape=jax.ShapeDtypeStruct((32, 128, 128)...  10.9 us
    unnamed x9, local copies, waits for them, and re-layouts  4.04 us

profile of v2, /device:TPU:2, one launch (start us, length us, event | category | flops | bytes accessed | tf_op | source)
XLA Modules:
  0.0 81.1 jit_solution(17666477853526576475)
XLA Ops:
  0.0 0.0 copy-start
  0.0 1.2 %copy-done = f32[16,16384]{1,0:T(8,128)S(1)} copy-done((f32[16,16384]{1,0:T(8,128)S(1)}, f32[16,16384]{1,0:T(8,128)}, u32[]{:S(2)}) %copy-start) | copy-done | bytes 1048600
  1.2 0.0 copy-start.1
  1.2 0.8 %copy-done.1 = s32[16384]{0:T(1024)S(1)} copy-done((s32[16384]{0:T(1024)S(1)}, s32[16384]{0:T(1024)}, u32[]{:S(2)}) %copy-start.1) | copy-done | bytes 65560
  2.1 0.0 copy-start.2
  2.1 0.7 copy-done.2
  2.8 0.0 copy-start.3
  2.8 0.7 copy-done.3
  3.4 42.6 %mix.1 = (f32[16,4,2,16,128]{4,3,2,1,0:T(8,128)S(1)}, s32[16,16,128]{2,1,0:T(8,128)S(1)}) custom-call(f32[16,16384]{1,0:T(8,128)S(1)} %copy-done, s32[128,128]{1,0:T(8,128)S(1)} %bitcast.8, s32[8,128]{1,0:T(8,128)S(1)} %bitcast.10, s32[8,128]{1,0:T(8,128)S(1)} %bitcast.11), custom_call_target="tpu_custom_call" | custom-call | tf_op jit(solution)/shard_map/mix/pallas_call | solution.py:313
  46.1 10.9 %gram.1 = f32[32,128,128]{2,1,0:T(8,128)S(1)} custom-call(f32[16,128,128]{2,1,0:T(8,128)S(1)} %bitcast.7, s32[16,16,128]{2,1,0:T(8,128)S(1)} %get-tuple-element.8.lists), custom_call_target="tpu_custom_call" | custom-call | tf_op jit(solution)/shard_map/gram/pallas_call | solution.py:333
  57.0 23.5 %sum.1 = f32[16,128]{1,0:T(8,128)S(1)} custom-call(f32[8,4,4,2,16,128]{5,4,3,2,1,0:T(8,128)S(1)} %bitcast.6), custom_call_target="tpu_custom_call" | custom-call | tf_op jit(solution)/shard_map/sum/pallas_call | solution.py:342
  80.5 0.6 copy.6
Async XLA Ops:
  0.0 1.2 %copy-start = (f32[16,16384]{1,0:T(8,128)S(1)}, f32[16,16384]{1,0:T(8,128)}, u32[]{:S(2)}) copy-start(f32[16,16384]{1,0:T(8,128)} %panel_hbm.1) | copy-start | bytes 3145732
  1.2 0.8 %copy-start.1 = (s32[16384]{0:T(1024)S(1)}, s32[16384]{0:T(1024)}, u32[]{:S(2)}) copy-start(s32[16384]{0:T(1024)} %param.5) | copy-start | bytes 196612
  2.1 0.7 copy-start.2
  2.8 0.7 copy-start.3

commit v3 on v2

--- a/solution.py
+++ b/solution.py
@@ -12,6 +12,7 @@
 BF16 = jnp.bfloat16
 NT = (((1,), (1,)), ((), ()))
 VMEM = pl.BlockSpec(memory_space=pltpu.VMEM)
+HBM = pl.BlockSpec(memory_space=pltpu.HBM)
 SLOTS = 32
 
 
@@ -75,8 +76,8 @@
 
 
 def mix_kernel(
-    panel_hbm, signs, offsets, owners, out, lists, panel, y_ref, r_ref, t_ref, mine,
-    load_sem, send_sem, recv_sem, core_send, core_recv, list_send, list_recv, plane_sem, all_sem,
+    panel_hbm, signs_hbm, offsets, owners, out, lists, panel, signs, y_ref, r_ref, t_ref, mine,
+    load_sem, small_sem, send_sem, recv_sem, core_send, core_recv, list_send, list_recv, plane_sem, all_sem,
 ):
     z, x, y, core = place()
     barrier = pltpu.get_barrier_semaphore()
@@ -86,13 +87,20 @@
         span = pl.ds(4096 * i, 4096)
         return pltpu.make_async_copy(panel_hbm.at[:, span], panel.at[:, span], load_sem.at[i])
 
+    small = [
+        pltpu.make_async_copy(signs_hbm, signs, small_sem.at[0]),
+        pltpu.make_async_copy(offsets, mine.at[pl.ds(0, 8)], small_sem.at[1]),
+        pltpu.make_async_copy(owners, mine.at[pl.ds(8, 8)], small_sem.at[2]),
+    ]
+    small[0].start()
     for i in range(4):
         load(i).start()
-    mine[0:8, :] = offsets[...]
-    mine[8:16, :] = owners[...]
+    small[1].start()
+    small[2].start()
     table = sylvester(128).astype(BF16)
     table = jnp.concatenate([table, table], axis=0)
 
+    small[0].wait()
     for part in range(4):
         load(part).wait()
         for i in range(2 * part, 2 * part + 2):
@@ -127,30 +135,43 @@
     to_y = [(y + d) % 4 for d in range(4)]
     sends_list = z // 4 == core
 
-    def send(i, carry):
+    small[1].wait()
+    small[2].wait()
+
+    def send(tz, dx, dy):
+        push(
+            y_ref.at[tz * 16 + to_x[dx] * 4 + to_y[dy]], r_ref.at[slot],
+            send_sem, recv_sem.at[dy], at(tz, to_x[dx], to_y[dy], core),
+        )
+
+    def send_list(tz, dx):
+        push(mine, lists.at[z % 4 * 4 + x], list_send, list_recv, at(tz, to_x[dx], y, core))
+
+    def first(i, carry):
         tz = (z + i * 3 + 4) % 8
         for g in range(2):
             vals = butterfly([y_ref[tz * 16 + g * 8 + j] for j in range(8)])
             for j in range(8):
                 y_ref[tz * 16 + g * 8 + j] = vals[j]
         for dx in range(4):
-            for dy in range(4):
-                def go():
-                    push(
-                        y_ref.at[tz * 16 + to_x[dx] * 4 + to_y[dy]], r_ref.at[slot],
-                        send_sem, recv_sem, at(tz, to_x[dx], to_y[dy], core),
-                    )
-                def go_list():
-                    push(mine, lists.at[z % 4 * 4 + x], list_send, list_recv, at(tz, to_x[dx], y, core))
-                if dx or dy:
-                    go()
-                else:
-                    pl.when(tz != z)(go)
-                if dy == 0:
-                    pl.when(sends_list if dx else sends_list & (tz != z))(go_list)
-        return carry
-
-    lax.fori_loop(0, 8, send, 0)
+            if dx:
+                send(tz, dx, 0)
+                pl.when(sends_list)(functools.partial(send_list, tz, dx))
+            else:
+                pl.when(tz != z)(functools.partial(send, tz, 0, 0))
+                pl.when(sends_list & (tz != z))(functools.partial(send_list, tz, 0))
+        return carry
+
+    lax.fori_loop(0, 8, first, 0)
+
+    for dy in range(1, 4):
+        def later(i, carry):
+            for dx in range(4):
+                send((z + i * 3 + 4) % 8, dx, dy)
+            return carry
+
+        lax.fori_loop(0, 8, later, 0)
+
     r_ref[slot] = y_ref[z * 16 + x * 4 + y]
 
     @pl.when(sends_list)
@@ -162,11 +183,10 @@
     def _():
         wait_bytes(lists, list_recv)
 
-    wait_bytes(r_ref.at[pl.ds(0, 127)], recv_sem)
-
     turn = (1 - 2 * core).astype(F32)
 
-    def across(v, carry):
+    def across(dy, carry):
+        v = (y + 4 - dy) % 4
         for h in range(2):
             rows = pl.ds(8 * h, 8)
             low = [r_ref[v * 32 + q, rows, :] for q in range(16)]
@@ -180,7 +200,14 @@
         push(t_ref.at[v], out.at[:, v, core], core_send, core_recv, at(z, x, y, 1 - core))
         return carry
 
-    lax.fori_loop(0, 4, across, 0)
+    wait_bytes(r_ref.at[pl.ds(0, 31)], recv_sem.at[0])
+    across(0, 0)
+
+    def across_next(dy, carry):
+        wait_bytes(r_ref.at[pl.ds(0, 32)], recv_sem.at[dy])
+        return across(dy, carry)
+
+    lax.fori_loop(1, 4, across_next, 0)
     wait_bytes(r_ref.at[pl.ds(0, 127)], send_sem)
 
     @pl.when(sends_list)
@@ -316,15 +343,16 @@
             jax.ShapeDtypeStruct((16, 4, 2, 16, 128), F32),
             jax.ShapeDtypeStruct((16, 16, 128), jnp.int32),
         ],
-        in_specs=[pl.BlockSpec(memory_space=pl.ANY)] + [VMEM] * 3,
+        in_specs=[HBM] * 4,
         out_specs=[VMEM] * 2,
         scratch_shapes=[
             pltpu.VMEM((16, 16384), F32),
+            pltpu.VMEM((128, 128), jnp.int32),
             pltpu.VMEM((128, 16, 128), F32),
             pltpu.VMEM((128, 16, 128), F32),
             pltpu.VMEM((4, 16, 16, 128), F32),
             pltpu.VMEM((16, 128), jnp.int32),
-            dma((4,)), dma, dma, dma, dma, dma, dma,
+            dma((4,)), dma((3,)), dma, dma((4,)), dma, dma, dma, dma,
             pltpu.SemaphoreType.REGULAR, pltpu.SemaphoreType.REGULAR,
         ],
         compiler_params=params(has_side_effects=True, collective_id=1),

time: 82.2 us -> 80.7 us (0.982)
  Pallas kernels: 77 us -> 75.7 us
    pallas_call x1, Pallas kernels: 42.6 us -> 40.9 us  [body(): pl.pallas_call(mix_kernel, out_shape=[jax.ShapeDtypeStruct((16, 4, 2, 16,...]
where the time goes in v3:
time: 80.7 us; the launch traced here: 79.7 us
  Pallas kernels  75.7 us (94%)
  local copies, waits for them, and re-layouts  4.04 us (5%)
    pallas_call x1, Pallas kernels, body(): pl.pallas_call(mix_kernel, out_shape=[jax.ShapeDtypeStruct((16, 4, 2, 16,...  40.9 us
    pallas_call x1, Pallas kernels, body(): pl.pallas_call(sum_kernel, out_shape=jax.ShapeDtypeStruct((16, 128), F32)...  23.8 us
    pallas_call x1, Pallas kernels, body(): pl.pallas_call(gram_kernel, out_shape=jax.ShapeDtypeStruct((32, 128, 128)...  10.9 us
    unnamed x9, local copies, waits for them, and re-layouts  4.04 us

profile of v3, /device:TPU:2, one launch (start us, length us, event | category | flops | bytes accessed | tf_op | source)
XLA Modules:
  0.0 79.7 jit_solution(504897265909303313)
XLA Ops:
  0.0 0.0 copy-start
  0.0 1.2 %copy-done = f32[16,16384]{1,0:T(8,128)S(1)} copy-done((f32[16,16384]{1,0:T(8,128)S(1)}, f32[16,16384]{1,0:T(8,128)}, u32[]{:S(2)}) %copy-start) | copy-done | bytes 1048600
  1.2 0.0 copy-start.1
  1.2 0.8 %copy-done.1 = s32[16384]{0:T(1024)S(1)} copy-done((s32[16384]{0:T(1024)S(1)}, s32[16384]{0:T(1024)}, u32[]{:S(2)}) %copy-start.1) | copy-done | bytes 65560
  2.1 0.0 copy-start.2
  2.1 0.7 copy-done.2
  2.8 0.0 copy-start.3
  2.8 0.7 copy-done.3
  3.4 40.9 %mix.1 = (f32[16,4,2,16,128]{4,3,2,1,0:T(8,128)S(1)}, s32[16,16,128]{2,1,0:T(8,128)S(1)}) custom-call(f32[16,16384]{1,0:T(8,128)S(1)} %copy-done, s32[128,128]{1,0:T(8,128)S(1)} %bitcast.8, s32[8,128]{1,0:T(8,128)S(1)} %bitcast.10, s32[8,128]{1,0:T(8,128)S(1)} %bitcast.11), custom_call_target="tpu_custom_call" | custom-call | tf_op jit(solution)/shard_map/mix/pallas_call | solution.py:340
  44.4 10.9 %gram.1 = f32[32,128,128]{2,1,0:T(8,128)S(1)} custom-call(f32[16,128,128]{2,1,0:T(8,128)S(1)} %bitcast.7, s32[16,16,128]{2,1,0:T(8,128)S(1)} %get-tuple-element.8.lists), custom_call_target="tpu_custom_call" | custom-call | tf_op jit(solution)/shard_map/gram/pallas_call | solution.py:361
  55.3 23.8 %sum.1 = f32[16,128]{1,0:T(8,128)S(1)} custom-call(f32[8,4,4,2,16,128]{5,4,3,2,1,0:T(8,128)S(1)} %bitcast.6), custom_call_target="tpu_custom_call" | custom-call | tf_op jit(solution)/shard_map/sum/pallas_call | solution.py:370
  79.1 0.6 copy.6
Async XLA Ops:
  0.0 1.2 %copy-start = (f32[16,16384]{1,0:T(8,128)S(1)}, f32[16,16384]{1,0:T(8,128)}, u32[]{:S(2)}) copy-start(f32[16,16384]{1,0:T(8,128)} %panel_hbm.1) | copy-start | bytes 3145732
  1.2 0.8 %copy-start.1 = (s32[16384]{0:T(1024)S(1)}, s32[16384]{0:T(1024)}, u32[]{:S(2)}) copy-start(s32[16384]{0:T(1024)} %param.5) | copy-start | bytes 196612
  2.1 0.7 copy-start.2
  2.8 0.7 copy-start.3

commit v4 on v3

--- a/solution.py
+++ b/solution.py
@@ -14,6 +14,8 @@
 VMEM = pl.BlockSpec(memory_space=pltpu.VMEM)
 HBM = pl.BlockSpec(memory_space=pltpu.HBM)
 SLOTS = 32
+MIX_VMEM = 60 << 20
+GRAM_SCALE = 2.0 ** -29
 
 
 def place():
@@ -76,8 +78,11 @@
 
 
 def mix_kernel(
-    panel_hbm, signs_hbm, offsets, owners, out, lists, panel, signs, y_ref, r_ref, t_ref, mine,
+    panel_hbm, signs_hbm, offsets, owners, result, crowded, lists, kept_hbm,
+    panel, signs, y_ref, r_ref, t_ref, mine, out, picks, names, picked, full_here, full_there,
+    g_ref, c_ref, ha, hb, a1, b1, sa, sb, a2, b2, sz, zr,
     load_sem, small_sem, send_sem, recv_sem, core_send, core_recv, list_send, list_recv, plane_sem, all_sem,
+    keep_sem, full_send, full_recv, s0, r0, s1, r1a, r1b, s2, r2a, r2b, s3, r3,
 ):
     z, x, y, core = place()
     barrier = pltpu.get_barrier_semaphore()
@@ -200,6 +205,24 @@
         push(t_ref.at[v], out.at[:, v, core], core_send, core_recv, at(z, x, y, 1 - core))
         return carry
 
+    rank, lane, name, seen = ranked(lists, z * 16 + x * 4 + y)
+    for g in range(4):
+        pick, its_name = chosen(rank, lane, name, g, 0.0)
+        picks[g] = pick
+        names[0:1, 128 * g : 128 * g + 128] = its_name
+
+    def tally(p, most):
+        slabs = lists[p, 0:8, :] // 128
+        count = jnp.zeros((128, 128), F32)
+        for b in range(8):
+            count = count + (slabs[b : b + 1, :] == iota((128, 128), 0)).astype(F32)
+        return jnp.maximum(most, jnp.sum(count, axis=1, keepdims=True))
+
+    most = lax.fori_loop(0, 16, tally, jnp.zeros((128, 1), F32))
+    most = jnp.max(most, axis=0, keepdims=True)
+    full_here[...] = jnp.broadcast_to(jnp.where(most > SLOTS, 1.0, 0.0), (8, 128))
+    push(full_here, full_there, full_send, full_recv, at(z, x, y, 1 - core))
+
     wait_bytes(r_ref.at[pl.ds(0, 31)], recv_sem.at[0])
     across(0, 0)
 
@@ -208,6 +231,71 @@
         return across(dy, carry)
 
     lax.fori_loop(1, 4, across_next, 0)
+    wait_bytes(t_ref, core_recv)
+    keep = pltpu.make_async_copy(out, kept_hbm, keep_sem)
+    keep.start()
+    for g in range(4):
+        got = jnp.dot(stacked(out, g), picks[g], preferred_element_type=F32)
+        picked[:, 128 * g : 128 * g + 128] = got.astype(BF16)
+
+    def make(i):
+        for tx in range(4):
+            total = owner_gram(picked[...], names[0:1, :], i * 4 + tx)
+            g_ref[i, tx] = total.reshape(4, 2, 16, 128)
+        push(g_ref.at[i, :, :, 1 - core], c_ref.at[i], s0, r0.at[i], at(z, x, y, 1 - core))
+
+    def forward(i):
+        wait_bytes(c_ref.at[i], r0.at[i])
+        for tx in range(4):
+            for ty in range(4):
+                ha[i, tx, ty] = g_ref[i, tx, ty, core, 0:8, :] + c_ref[i, tx, ty, 0:8, :]
+                hb[i, ty, tx] = g_ref[i, tx, ty, core, 8:16, :] + c_ref[i, tx, ty, 8:16, :]
+        for d in (2, 1, 3):
+            push(ha.at[i, to_x[d]], a1.at[x, i], s1.at[0], r1a.at[i // 4], at(z, to_x[d], y, core))
+            push(hb.at[i, to_y[d]], b1.at[y, i], s1.at[1], r1b.at[i // 4], at(z, x, to_y[d], core))
+        a1[x, i] = ha[i, x]
+        b1[y, i] = hb[i, y]
+
+    def step(i, carry):
+        make(i)
+        forward(i - 1)
+        return carry
+
+    make(jnp.int32(0))
+    lax.fori_loop(1, 8, step, 0)
+    forward(jnp.int32(7))
+
+    for h in range(2):
+        wait_bytes(a1.at[pl.ds(0, 3), pl.ds(0, 4)], r1a.at[h])
+        wait_bytes(b1.at[pl.ds(0, 3), pl.ds(0, 4)], r1b.at[h])
+        for i in range(4):
+            for t in range(4):
+                n = 4 * h + i
+                sa[h, t, i] = (a1[0, n, t] + a1[1, n, t]) + (a1[2, n, t] + a1[3, n, t])
+                sb[h, t, i] = (b1[0, n, t] + b1[1, n, t]) + (b1[2, n, t] + b1[3, n, t])
+        for d in (2, 1, 3):
+            push(sa.at[h, to_y[d]], a2.at[h, y], s2.at[0], r2a.at[h], at(z, x, to_y[d], core))
+            push(sb.at[h, to_x[d]], b2.at[h, x], s2.at[1], r2b.at[h], at(z, to_x[d], y, core))
+        a2[h, y] = sa[h, y]
+        b2[h, x] = sb[h, x]
+
+    for h in range(2):
+        wait_bytes(a2.at[h, pl.ds(0, 3)], r2a.at[h])
+        wait_bytes(b2.at[h, pl.ds(0, 3)], r2b.at[h])
+        for i in range(4):
+            n = 4 * h + i
+            sz[n, 0:8, :] = (a2[h, 0, i] + a2[h, 1, i]) + (a2[h, 2, i] + a2[h, 3, i])
+            sz[n, 8:16, :] = (b2[h, 0, i] + b2[h, 1, i]) + (b2[h, 2, i] + b2[h, 3, i])
+            pl.when(z != n)(functools.partial(push, sz.at[n], zr.at[z], s3, r3, at(n, x, y, core)))
+
+    zr[z] = sz[z]
+    wait_bytes(zr.at[pl.ds(0, 7)], r3)
+    v = [zr[i] for i in range(8)]
+    total = ((v[0] + v[1]) + (v[2] + v[3])) + ((v[4] + v[5]) + (v[6] + v[7]))
+    result[...] = total * GRAM_SCALE
+    wait_bytes(full_there, full_recv)
+    crowded[...] = jnp.maximum(full_here[...], full_there[...])
+
     wait_bytes(r_ref.at[pl.ds(0, 127)], send_sem)
 
     @pl.when(sends_list)
@@ -215,17 +303,18 @@
         for n in range(31):
             wait_bytes(mine, list_send)
 
+    keep.wait()
+    wait_bytes(full_here, full_send)
     wait_bytes(t_ref, core_send)
-    wait_bytes(t_ref, core_recv)
-
-
-def gram_kernel(mixed, lists, out, wide, picked):
-    z, x, y, core = place()
-    slab = z * 16 + x * 4 + y
-    for p in range(16):
-        hi, lo = split(mixed[p])
-        wide[0:128, 128 * p : 128 * p + 128] = hi
-        wide[128:256, 128 * p : 128 * p + 128] = lo
+    wait_bytes(c_ref, s0)
+    wait_bytes(a1.at[pl.ds(0, 3)], s1.at[0])
+    wait_bytes(b1.at[pl.ds(0, 3)], s1.at[1])
+    wait_bytes(a2.at[:, pl.ds(0, 3)], s2.at[0])
+    wait_bytes(b2.at[:, pl.ds(0, 3)], s2.at[1])
+    wait_bytes(zr.at[pl.ds(0, 7)], s3)
+
+
+def ranked(lists, slab):
     here = jnp.concatenate([lists[:, b, :] for b in range(8)], axis=1) - slab * 128
     owner = jnp.concatenate([lists[:, 8 + b, :] for b in range(8)], axis=1)
     inside = (here >= 0) & (here < 128)
@@ -236,44 +325,65 @@
         piece = mask[:, 128 * b : 128 * b + 128]
         rank.append(jnp.dot(piece.astype(BF16), before, preferred_element_type=F32) + seen)
         seen = seen + jnp.sum(piece, axis=1, keepdims=True)
-    rank = jnp.where(inside, jnp.concatenate(rank, axis=1), -1.0).astype(jnp.int32)
+    rank = jnp.where(inside, jnp.concatenate(rank, axis=1), -1.0)
     lane = jnp.where(inside, here, 0).astype(F32)
     name = jnp.where(inside, owner + 1, 0).astype(F32)
+    return rank, lane, name, seen
+
+
+def chosen(rank, lane, name, g, first):
+    wanted = iota((SLOTS, 1024), 0).astype(F32) + first
+    hot = [rank[p : p + 1, :] == wanted for p in range(4 * g, 4 * g + 4)]
+    hot = jnp.concatenate([h.astype(F32) for h in hot], axis=0).astype(BF16)
+    facts = jnp.concatenate([lane[4 * g : 4 * g + 4], name[4 * g : 4 * g + 4]], axis=0)
+    found = lax.dot_general(facts.astype(BF16), hot, NT, preferred_element_type=F32)
+    which = iota((1, 128), 1) // SLOTS
+    at_lane, its_name = jnp.zeros((1, 128), F32), jnp.zeros((1, 128), F32)
+    for p in range(4):
+        at_lane = jnp.where(which == p, found[p : p + 1, :] + 128.0 * p, at_lane)
+        its_name = jnp.where(which == p, found[4 + p : 5 + p, :], its_name)
+    spot = jnp.where(its_name > 0.5, at_lane, -1.0)
+    pick = (iota((512, 128), 0).astype(F32) == spot).astype(F32).astype(BF16)
+    return pick, its_name
+
+
+def stacked(mixed, g):
+    columns = []
+    for p in range(4 * g, 4 * g + 4):
+        hi, lo = split(mixed[p].reshape(128, 128))
+        columns.append(jnp.concatenate([hi, lo], axis=0))
+    return jnp.concatenate(columns, axis=1)
+
+
+def owner_gram(picked, names, o):
+    member = (names == o.astype(F32) + 1.0).astype(F32).astype(BF16)
+    both = lax.dot_general(picked * member, picked, NT, preferred_element_type=F32)
+    return (both[:128, :128] + both[128:, 128:]) + (both[:128, 128:] + both[128:, :128])
+
+
+def gram_kernel(mixed, lists, out, picked):
+    z, x, y, core = place()
+    rank, lane, name, seen = ranked(lists, z * 16 + x * 4 + y)
     rounds = (jnp.max(seen).astype(jnp.int32) + SLOTS - 1) // SLOTS
     out[...] = jnp.zeros_like(out)
 
     def one_round(r, carry):
         names = []
         for g in range(4):
-            hot = []
-            for p in range(4 * g, 4 * g + 4):
-                hot.append(rank[p : p + 1, :] == iota((SLOTS, 1024), 0) + r * SLOTS)
-            hot = jnp.concatenate(hot, axis=0).astype(F32).astype(BF16)
-            facts = jnp.concatenate([lane[4 * g : 4 * g + 4], name[4 * g : 4 * g + 4]], axis=0)
-            found = lax.dot_general(facts.astype(BF16), hot, NT, preferred_element_type=F32)
-            which = iota((1, 128), 1) // SLOTS
-            at_lane, its_name = jnp.zeros((1, 128), F32), jnp.zeros((1, 128), F32)
-            for p in range(4):
-                at_lane = jnp.where(which == p, found[p : p + 1, :], at_lane)
-                its_name = jnp.where(which == p, found[4 + p : 5 + p, :], its_name)
-            spot = jnp.where(its_name > 0.5, at_lane.astype(jnp.int32) + which * 128, -1)
-            pick = (iota((512, 128), 0) == spot).astype(F32).astype(BF16)
-            got = jnp.dot(wide[:, 512 * g : 512 * g + 512], pick, preferred_element_type=F32)
+            pick, its_name = chosen(rank, lane, name, g, (r * SLOTS).astype(F32))
+            got = jnp.dot(stacked(mixed, g), pick, preferred_element_type=F32)
             picked[:, 128 * g : 128 * g + 128] = got.astype(BF16)
             names.append(its_name)
         names = jnp.concatenate(names, axis=1)
 
         def one_owner(o, carry):
-            member = (names == (o + 1).astype(F32)).astype(F32).astype(BF16)
-            both = lax.dot_general(picked[...] * member, picked[...], NT, preferred_element_type=F32)
-            total = (both[:128, :128] + both[128:, 128:]) + (both[:128, 128:] + both[128:, :128])
-            out[o] += total * (2.0 ** -29)
+            out[o] += owner_gram(picked[...], names, o) * GRAM_SCALE
             return carry
 
         lax.fori_loop(0, 32, one_owner, 0)
         return carry
 
-    lax.fori_loop(0, rounds, one_round, 0)
+    lax.fori_loop(1, rounds, one_round, 0)
 
 
 def sum_kernel(gram, out, c_ref, ha, hb, a1, b1, sa, sb, a2, b2, sz, zr, s0, r0, s1, r1, s2, r2, s3, r3):
@@ -335,60 +445,86 @@
 
 
 def body(panel, signs, offsets, owners):
-    params = functools.partial(pltpu.CompilerParams, vmem_limit_bytes=48 << 20)
-    dma = pltpu.SemaphoreType.DMA
-    mixed, lists = pl.pallas_call(
+    params = functools.partial(pltpu.CompilerParams, has_side_effects=True)
+    dma, vmem = pltpu.SemaphoreType.DMA, pltpu.VMEM
+    result, crowded, lists, mixed = pl.pallas_call(
         mix_kernel,
         out_shape=[
+            jax.ShapeDtypeStruct((16, 128), F32),
+            jax.ShapeDtypeStruct((8, 128), F32),
+            jax.ShapeDtypeStruct((16, 16, 128), jnp.int32),
             jax.ShapeDtypeStruct((16, 4, 2, 16, 128), F32),
-            jax.ShapeDtypeStruct((16, 16, 128), jnp.int32),
         ],
         in_specs=[HBM] * 4,
-        out_specs=[VMEM] * 2,
+        out_specs=[VMEM] * 3 + [HBM],
         scratch_shapes=[
-            pltpu.VMEM((16, 16384), F32),
-            pltpu.VMEM((128, 128), jnp.int32),
-            pltpu.VMEM((128, 16, 128), F32),
-            pltpu.VMEM((128, 16, 128), F32),
-            pltpu.VMEM((4, 16, 16, 128), F32),
-            pltpu.VMEM((16, 128), jnp.int32),
+            vmem((16, 16384), F32),
+            vmem((128, 128), jnp.int32),
+            vmem((128, 16, 128), F32),
+            vmem((128, 16, 128), F32),
+            vmem((4, 16, 16, 128), F32),
+            vmem((16, 128), jnp.int32),
+            vmem((16, 4, 2, 16, 128), F32),
+            vmem((4, 512, 128), BF16),
+            vmem((8, 512), F32),
+            vmem((256, 512), BF16),
+            vmem((8, 128), F32),
+            vmem((8, 128), F32),
+            vmem((8, 4, 4, 2, 16, 128), F32),
+            vmem((8, 4, 4, 16, 128), F32),
+            vmem((8, 4, 4, 8, 128), F32),
+            vmem((8, 4, 4, 8, 128), F32),
+            vmem((4, 8, 4, 8, 128), F32),
+            vmem((4, 8, 4, 8, 128), F32),
+            vmem((2, 4, 4, 8, 128), F32),
+            vmem((2, 4, 4, 8, 128), F32),
+            vmem((2, 4, 4, 8, 128), F32),
+            vmem((2, 4, 4, 8, 128), F32),
+            vmem((8, 16, 128), F32),
+            vmem((8, 16, 128), F32),
             dma((4,)), dma((3,)), dma, dma((4,)), dma, dma, dma, dma,
             pltpu.SemaphoreType.REGULAR, pltpu.SemaphoreType.REGULAR,
+            dma, dma, dma, dma, dma((8,)), dma((2,)), dma((2,)), dma((2,)),
+            dma((2,)), dma((2,)), dma((2,)), dma, dma,
         ],
-        compiler_params=params(has_side_effects=True, collective_id=1),
+        compiler_params=params(collective_id=1, vmem_limit_bytes=MIX_VMEM),
         name="mix",
     )(panel, signs.reshape(128, 128), offsets.reshape(8, 128), owners.reshape(8, 128))
-    gram = pl.pallas_call(
-        gram_kernel,
-        out_shape=jax.ShapeDtypeStruct((32, 128, 128), F32),
-        in_specs=[VMEM] * 2,
-        out_specs=VMEM,
-        scratch_shapes=[pltpu.VMEM((256, 2048), BF16), pltpu.VMEM((256, 512), BF16)],
-        compiler_params=params(),
-        name="gram",
-    )(mixed.reshape(16, 128, 128), lists)
-    summed = pl.pallas_call(
-        sum_kernel,
-        out_shape=jax.ShapeDtypeStruct((16, 128), F32),
-        in_specs=[VMEM],
-        out_specs=VMEM,
-        scratch_shapes=[
-            pltpu.VMEM((8, 4, 4, 16, 128), F32),
-            pltpu.VMEM((4, 8, 4, 8, 128), F32),
-            pltpu.VMEM((4, 8, 4, 8, 128), F32),
-            pltpu.VMEM((4, 8, 4, 8, 128), F32),
-            pltpu.VMEM((4, 8, 4, 8, 128), F32),
-            pltpu.VMEM((4, 8, 8, 128), F32),
-            pltpu.VMEM((4, 8, 8, 128), F32),
-            pltpu.VMEM((4, 8, 8, 128), F32),
-            pltpu.VMEM((4, 8, 8, 128), F32),
-            pltpu.VMEM((8, 16, 128), F32),
-            pltpu.VMEM((8, 16, 128), F32),
-        ] + [dma] * 2 + [dma((2,))] * 4 + [dma] * 2,
-        compiler_params=params(has_side_effects=True, collective_id=2),
-        name="sum",
-    )(gram.reshape(8, 4, 4, 2, 16, 128))
-    return summed[None]
+
+    def add_rest(result):
+        gram = pl.pallas_call(
+            gram_kernel,
+            out_shape=jax.ShapeDtypeStruct((32, 128, 128), F32),
+            in_specs=[VMEM] * 2,
+            out_specs=VMEM,
+            scratch_shapes=[vmem((256, 512), BF16)],
+            compiler_params=pltpu.CompilerParams(vmem_limit_bytes=48 << 20),
+            name="gram_rest",
+        )(mixed.reshape(16, 128, 128), lists)
+        rest = pl.pallas_call(
+            sum_kernel,
+            out_shape=jax.ShapeDtypeStruct((16, 128), F32),
+            in_specs=[VMEM],
+            out_specs=VMEM,
+            scratch_shapes=[
+                vmem((8, 4, 4, 16, 128), F32),
+                vmem((4, 8, 4, 8, 128), F32),
+                vmem((4, 8, 4, 8, 128), F32),
+                vmem((4, 8, 4, 8, 128), F32),
+                vmem((4, 8, 4, 8, 128), F32),
+                vmem((4, 8, 8, 128), F32),
+                vmem((4, 8, 8, 128), F32),
+                vmem((4, 8, 8, 128), F32),
+                vmem((4, 8, 8, 128), F32),
+                vmem((8, 16, 128), F32),
+                vmem((8, 16, 128), F32),
+            ] + [dma] * 2 + [dma((2,))] * 4 + [dma] * 2,
+            compiler_params=params(collective_id=2, vmem_limit_bytes=48 << 20),
+            name="sum_rest",
+        )(gram.reshape(8, 4, 4, 2, 16, 128))
+        return result + rest
+
+    return lax.cond(crowded[0, 0] > 0.5, add_rest, lambda r: r, result)[None]
 
 
 def solution(mesh):

time: 80.7 us -> 63.1 us (0.78)
  Pallas kernels: 75.7 us -> 59.9 us
  local copies, waits for them, and re-layouts: 4.04 us -> 1.79 us
    pallas_call x3 -> x1, Pallas kernels: 75.7 us -> 59.9 us  [body(): pl.pallas_call(mix_kernel, out_shape=[jax.ShapeDtypeStruct((16, 128), F32...]
    unnamed x9 -> x1, local copies, waits for them, and re-layouts: 4.04 us -> 0.6 us
    slice x0 -> x1, local copies, waits for them, and re-layouts: none -> 1.19 us  [body(): return lax.cond(crowded[0, 0] > 0.5, add_rest, lambda r: r, result)[None]]
where the time goes in v4:
time: 63.1 us; the launch traced here: 62.4 us
  Pallas kernels  59.9 us (95%)
  local copies, waits for them, and re-layouts  1.79 us (3%)
  between operations  0.67 us (1%)
    pallas_call x1, Pallas kernels, body(): pl.pallas_call(mix_kernel, out_shape=[jax.ShapeDtypeStruct((16, 128), F32...  59.9 us

profile of v4, /device:TPU:2, one launch (start us, length us, event | category | flops | bytes accessed | tf_op | source)
XLA Modules:
  0.0 62.4 jit_solution(10610375142316850886)
XLA Ops:
  0.0 59.9 %mix.1 = (f32[16,128]{1,0:T(8,128)S(1)}, f32[8,128]{1,0:T(8,128)}, s32[16,16,128]{2,1,0:T(8,128)S(1)}, f32[16,4,2,16,128]{4,3,2,1,0:T(8,128)S(1)}) custom-call(f32[16,16384]{1,0:T(8,128)} %panel_hbm.1, s32[128,128]{1,0:T(8,128)} %bitcast.11, s32[8,128]{1,0:T(8,128)} %bitcast.13, s32[8,128]{1,0:T(8,128)} %bitcast.14), custom_call_target="tpu_custom_call" | custom-call | tf_op jit(solution)/shard_map/mix/pallas_call | solution.py:450
  59.9 1.2 %slice.3 = f32[1,1]{1,0:T(1,128)} slice(f32[8,128]{1,0:T(8,128)} %get-tuple-element.24), slice={[0:1], [0:1]} | slice | bytes 8 | tf_op jit(solution)/shard_map/slice | solution.py:527
  61.8 0.6 copy.11
  (1 shorter events, 0.0 us)

commit v5 on v4

--- a/solution.py
+++ b/solution.py
@@ -12,8 +12,10 @@
 BF16 = jnp.bfloat16
 NT = (((1,), (1,)), ((), ()))
 VMEM = pl.BlockSpec(memory_space=pltpu.VMEM)
+SMEM = pl.BlockSpec(memory_space=pltpu.SMEM)
 HBM = pl.BlockSpec(memory_space=pltpu.HBM)
 SLOTS = 32
+TAKEN = 256
 MIX_VMEM = 60 << 20
 GRAM_SCALE = 2.0 ** -29
 
@@ -79,7 +81,7 @@
 
 def mix_kernel(
     panel_hbm, signs_hbm, offsets, owners, result, crowded, lists, kept_hbm,
-    panel, signs, y_ref, r_ref, t_ref, mine, out, picks, names, picked, full_here, full_there,
+    panel, signs, y_ref, r_ref, t_ref, mine, out, lanes, ids, ranks, picks, names, picked, full_here, full_there,
     g_ref, c_ref, ha, hb, a1, b1, sa, sb, a2, b2, sz, zr,
     load_sem, small_sem, send_sem, recv_sem, core_send, core_recv, list_send, list_recv, plane_sem, all_sem,
     keep_sem, full_send, full_recv, s0, r0, s1, r1a, r1b, s2, r2a, r2b, s3, r3,
@@ -206,21 +208,43 @@
         return carry
 
     rank, lane, name, seen = ranked(lists, z * 16 + x * 4 + y)
-    for g in range(4):
-        pick, its_name = chosen(rank, lane, name, g, 0.0)
-        picks[g] = pick
-        names[0:1, 128 * g : 128 * g + 128] = its_name
-
-    def tally(p, most):
+    lanes[...], ids[...] = lane, name
+    ahead = jnp.zeros((1, 1), F32)
+    for p in range(16):
+        row = rank[p : p + 1, :]
+        ranks[p : p + 1, :] = jnp.where(row >= 0.0, row + ahead, -1.0)
+        ahead = ahead + seen[p : p + 1, :]
+
+    def locate(p, carry):
+        spot, its_name = carry
+        one = pl.ds(p, 1)
+        hot = (iota((TAKEN, 1024), 0).astype(F32) == ranks[one, :]).astype(F32).astype(BF16)
+        facts = jnp.concatenate([lanes[one, :], ids[one, :], jnp.zeros((6, 1024), F32)], axis=0)
+        found = lax.dot_general(facts.astype(BF16), hot, NT, preferred_element_type=F32)
+        base = (p * 128).astype(F32)
+        spot = jnp.where(found[1:2, :] > 0.5, found[0:1, :] + base, spot)
+        return spot, its_name + found[1:2, :]
+
+    nowhere = jnp.zeros((1, TAKEN), F32)
+    spot, its_name = lax.fori_loop(0, 16, locate, (nowhere - 1.0, nowhere))
+    names[0:1, :] = its_name
+
+    def mark(k, carry):
+        rows = iota((256, TAKEN), 0).astype(F32) + (k * 256).astype(F32)
+        picks[k] = (rows == spot).astype(F32).astype(BF16)
+        return carry
+
+    lax.fori_loop(0, 8, mark, 0)
+
+    def tally(p, count):
         slabs = lists[p, 0:8, :] // 128
-        count = jnp.zeros((128, 128), F32)
         for b in range(8):
             count = count + (slabs[b : b + 1, :] == iota((128, 128), 0)).astype(F32)
-        return jnp.maximum(most, jnp.sum(count, axis=1, keepdims=True))
-
-    most = lax.fori_loop(0, 16, tally, jnp.zeros((128, 1), F32))
-    most = jnp.max(most, axis=0, keepdims=True)
-    full_here[...] = jnp.broadcast_to(jnp.where(most > SLOTS, 1.0, 0.0), (8, 128))
+        return count
+
+    count = lax.fori_loop(0, 16, tally, jnp.zeros((128, 128), F32))
+    most = jnp.max(jnp.sum(count, axis=1, keepdims=True), axis=0, keepdims=True)
+    full_here[...] = jnp.broadcast_to(jnp.where(most > TAKEN, 1, 0), (8, 128))
     push(full_here, full_there, full_send, full_recv, at(z, x, y, 1 - core))
 
     wait_bytes(r_ref.at[pl.ds(0, 31)], recv_sem.at[0])
@@ -234,14 +258,22 @@
     wait_bytes(t_ref, core_recv)
     keep = pltpu.make_async_copy(out, kept_hbm, keep_sem)
     keep.start()
+    got = jnp.zeros((256, TAKEN), F32)
     for g in range(4):
-        got = jnp.dot(stacked(out, g), picks[g], preferred_element_type=F32)
-        picked[:, 128 * g : 128 * g + 128] = got.astype(BF16)
+        pick = picks[2 * g : 2 * g + 2].reshape(512, TAKEN)
+        got = got + jnp.dot(stacked(out, g), pick, preferred_element_type=F32)
+    picked[...] = got.astype(BF16)
 
     def make(i):
+        whole = picked[...]
+        members = []
         for tx in range(4):
-            total = owner_gram(picked[...], names[0:1, :], i * 4 + tx)
-            g_ref[i, tx] = total.reshape(4, 2, 16, 128)
+            wanted = (i * 4 + tx + 1).astype(F32)
+            members.append(whole * (names[0:1, :] == wanted).astype(F32).astype(BF16))
+        members = jnp.concatenate(members, axis=0)
+        both = lax.dot_general(members, whole, NT, preferred_element_type=F32)
+        for tx in range(4):
+            g_ref[i, tx] = folded(both[256 * tx : 256 * tx + 256]).reshape(4, 2, 16, 128)
         push(g_ref.at[i, :, :, 1 - core], c_ref.at[i], s0, r0.at[i], at(z, x, y, 1 - core))
 
     def forward(i):
@@ -251,26 +283,17 @@
                 ha[i, tx, ty] = g_ref[i, tx, ty, core, 0:8, :] + c_ref[i, tx, ty, 0:8, :]
                 hb[i, ty, tx] = g_ref[i, tx, ty, core, 8:16, :] + c_ref[i, tx, ty, 8:16, :]
         for d in (2, 1, 3):
-            push(ha.at[i, to_x[d]], a1.at[x, i], s1.at[0], r1a.at[i // 4], at(z, to_x[d], y, core))
-            push(hb.at[i, to_y[d]], b1.at[y, i], s1.at[1], r1b.at[i // 4], at(z, x, to_y[d], core))
+            push(ha.at[i, to_x[d]], a1.at[x, i], s1.at[0], r1a.at[i // 2], at(z, to_x[d], y, core))
+            push(hb.at[i, to_y[d]], b1.at[y, i], s1.at[1], r1b.at[i // 2], at(z, x, to_y[d], core))
         a1[x, i] = ha[i, x]
         b1[y, i] = hb[i, y]
 
-    def step(i, carry):
-        make(i)
-        forward(i - 1)
-        return carry
-
-    make(jnp.int32(0))
-    lax.fori_loop(1, 8, step, 0)
-    forward(jnp.int32(7))
-
-    for h in range(2):
-        wait_bytes(a1.at[pl.ds(0, 3), pl.ds(0, 4)], r1a.at[h])
-        wait_bytes(b1.at[pl.ds(0, 3), pl.ds(0, 4)], r1b.at[h])
-        for i in range(4):
+    def second(h):
+        wait_bytes(a1.at[pl.ds(0, 3), pl.ds(0, 2)], r1a.at[h])
+        wait_bytes(b1.at[pl.ds(0, 3), pl.ds(0, 2)], r1b.at[h])
+        for i in range(2):
             for t in range(4):
-                n = 4 * h + i
+                n = 2 * h + i
                 sa[h, t, i] = (a1[0, n, t] + a1[1, n, t]) + (a1[2, n, t] + a1[3, n, t])
                 sb[h, t, i] = (b1[0, n, t] + b1[1, n, t]) + (b1[2, n, t] + b1[3, n, t])
         for d in (2, 1, 3):
@@ -279,22 +302,32 @@
         a2[h, y] = sa[h, y]
         b2[h, x] = sb[h, x]
 
-    for h in range(2):
+    def third(h):
         wait_bytes(a2.at[h, pl.ds(0, 3)], r2a.at[h])
         wait_bytes(b2.at[h, pl.ds(0, 3)], r2b.at[h])
-        for i in range(4):
-            n = 4 * h + i
+        for i in range(2):
+            n = 2 * h + i
             sz[n, 0:8, :] = (a2[h, 0, i] + a2[h, 1, i]) + (a2[h, 2, i] + a2[h, 3, i])
             sz[n, 8:16, :] = (b2[h, 0, i] + b2[h, 1, i]) + (b2[h, 2, i] + b2[h, 3, i])
             pl.when(z != n)(functools.partial(push, sz.at[n], zr.at[z], s3, r3, at(n, x, y, core)))
 
+    def step(j, carry):
+        pl.when(j < 4)(functools.partial(make, 2 * j))
+        pl.when((j >= 1) & (j < 5))(functools.partial(forward, 2 * j - 2))
+        pl.when(j < 4)(functools.partial(make, 2 * j + 1))
+        pl.when((j >= 1) & (j < 5))(functools.partial(forward, 2 * j - 1))
+        pl.when((j >= 2) & (j < 6))(functools.partial(second, j - 2))
+        pl.when(j >= 3)(functools.partial(third, j - 3))
+        return carry
+
+    lax.fori_loop(0, 7, step, 0)
     zr[z] = sz[z]
     wait_bytes(zr.at[pl.ds(0, 7)], r3)
     v = [zr[i] for i in range(8)]
     total = ((v[0] + v[1]) + (v[2] + v[3])) + ((v[4] + v[5]) + (v[6] + v[7]))
     result[...] = total * GRAM_SCALE
     wait_bytes(full_there, full_recv)
-    crowded[...] = jnp.maximum(full_here[...], full_there[...])
+    crowded[0, 0] = jnp.max(jnp.maximum(full_here[...], full_there[...]))
 
     wait_bytes(r_ref.at[pl.ds(0, 127)], send_sem)
 
@@ -355,10 +388,14 @@
     return jnp.concatenate(columns, axis=1)
 
 
+def folded(both):
+    return (both[:128, :128] + both[128:, 128:]) + (both[:128, 128:] + both[128:, :128])
+
+
 def owner_gram(picked, names, o):
     member = (names == o.astype(F32) + 1.0).astype(F32).astype(BF16)
     both = lax.dot_general(picked * member, picked, NT, preferred_element_type=F32)
-    return (both[:128, :128] + both[128:, 128:]) + (both[:128, 128:] + both[128:, :128])
+    return folded(both)
 
 
 def gram_kernel(mixed, lists, out, picked):
@@ -383,7 +420,7 @@
         lax.fori_loop(0, 32, one_owner, 0)
         return carry
 
-    lax.fori_loop(1, rounds, one_round, 0)
+    lax.fori_loop(0, rounds, one_round, 0)
 
 
 def sum_kernel(gram, out, c_ref, ha, hb, a1, b1, sa, sb, a2, b2, sz, zr, s0, r0, s1, r1, s2, r2, s3, r3):
@@ -451,12 +488,12 @@
         mix_kernel,
         out_shape=[
             jax.ShapeDtypeStruct((16, 128), F32),
-            jax.ShapeDtypeStruct((8, 128), F32),
+            jax.ShapeDtypeStruct((1, 1), jnp.int32),
             jax.ShapeDtypeStruct((16, 16, 128), jnp.int32),
             jax.ShapeDtypeStruct((16, 4, 2, 16, 128), F32),
         ],
         in_specs=[HBM] * 4,
-        out_specs=[VMEM] * 3 + [HBM],
+        out_specs=[VMEM, SMEM, VMEM, HBM],
         scratch_shapes=[
             vmem((16, 16384), F32),
             vmem((128, 128), jnp.int32),
@@ -465,33 +502,36 @@
             vmem((4, 16, 16, 128), F32),
             vmem((16, 128), jnp.int32),
             vmem((16, 4, 2, 16, 128), F32),
-            vmem((4, 512, 128), BF16),
-            vmem((8, 512), F32),
-            vmem((256, 512), BF16),
-            vmem((8, 128), F32),
-            vmem((8, 128), F32),
+            vmem((16, 1024), F32),
+            vmem((16, 1024), F32),
+            vmem((16, 1024), F32),
+            vmem((8, 256, TAKEN), BF16),
+            vmem((8, TAKEN), F32),
+            vmem((256, TAKEN), BF16),
+            vmem((8, 128), jnp.int32),
+            vmem((8, 128), jnp.int32),
             vmem((8, 4, 4, 2, 16, 128), F32),
             vmem((8, 4, 4, 16, 128), F32),
             vmem((8, 4, 4, 8, 128), F32),
             vmem((8, 4, 4, 8, 128), F32),
             vmem((4, 8, 4, 8, 128), F32),
             vmem((4, 8, 4, 8, 128), F32),
-            vmem((2, 4, 4, 8, 128), F32),
-            vmem((2, 4, 4, 8, 128), F32),
-            vmem((2, 4, 4, 8, 128), F32),
-            vmem((2, 4, 4, 8, 128), F32),
+            vmem((4, 4, 2, 8, 128), F32),
+            vmem((4, 4, 2, 8, 128), F32),
+            vmem((4, 4, 2, 8, 128), F32),
+            vmem((4, 4, 2, 8, 128), F32),
             vmem((8, 16, 128), F32),
             vmem((8, 16, 128), F32),
             dma((4,)), dma((3,)), dma, dma((4,)), dma, dma, dma, dma,
             pltpu.SemaphoreType.REGULAR, pltpu.SemaphoreType.REGULAR,
-            dma, dma, dma, dma, dma((8,)), dma((2,)), dma((2,)), dma((2,)),
-            dma((2,)), dma((2,)), dma((2,)), dma, dma,
+            dma, dma, dma, dma, dma((8,)), dma((2,)), dma((4,)), dma((4,)),
+            dma((2,)), dma((4,)), dma((4,)), dma, dma,
         ],
         compiler_params=params(collective_id=1, vmem_limit_bytes=MIX_VMEM),
         name="mix",
     )(panel, signs.reshape(128, 128), offsets.reshape(8, 128), owners.reshape(8, 128))
 
-    def add_rest(result):
+    def in_rounds():
         gram = pl.pallas_call(
             gram_kernel,
             out_shape=jax.ShapeDtypeStruct((32, 128, 128), F32),
@@ -499,9 +539,9 @@
             out_specs=VMEM,
             scratch_shapes=[vmem((256, 512), BF16)],
             compiler_params=pltpu.CompilerParams(vmem_limit_bytes=48 << 20),
-            name="gram_rest",
+            name="gram_rounds",
         )(mixed.reshape(16, 128, 128), lists)
-        rest = pl.pallas_call(
+        return pl.pallas_call(
             sum_kernel,
             out_shape=jax.ShapeDtypeStruct((16, 128), F32),
             in_specs=[VMEM],
@@ -520,11 +560,10 @@
                 vmem((8, 16, 128), F32),
             ] + [dma] * 2 + [dma((2,))] * 4 + [dma] * 2,
             compiler_params=params(collective_id=2, vmem_limit_bytes=48 << 20),
-            name="sum_rest",
+            name="sum_rounds",
         )(gram.reshape(8, 4, 4, 2, 16, 128))
-        return result + rest
-
-    return lax.cond(crowded[0, 0] > 0.5, add_rest, lambda r: r, result)[None]
+
+    return lax.cond(crowded[0, 0] > 0, in_rounds, lambda: result)[None]
 
 
 def solution(mesh):

time: 63.1 us -> 63.2 us (level)
  Pallas kernels: 59.9 us -> 61.9 us
  local copies, waits for them, and re-layouts: 1.79 us -> 0.6 us
    pallas_call x1, Pallas kernels: 59.9 us -> 61.9 us  [body(): pl.pallas_call(mix_kernel, out_shape=[jax.ShapeDtypeStruct((16, 128), F32...]
    slice x1 -> x0, local copies, waits for them, and re-layouts: 1.19 us -> none  [body(): return lax.cond(crowded[0, 0] > 0.5, add_rest, lambda r: r, result)[None]]
where the time goes in v5:
time: 63.2 us; the launch traced here: 63.1 us
  Pallas kernels  61.9 us (98%)
  between operations  0.65 us (1%)
    pallas_call x1, Pallas kernels, body(): pl.pallas_call(mix_kernel, out_shape=[jax.ShapeDtypeStruct((16, 128), F32...  61.9 us

profile of v5, /device:TPU:2, one launch (start us, length us, event | category | flops | bytes accessed | tf_op | source)
XLA Modules:
  0.0 63.1 jit_solution(13287579174642586957)
XLA Ops:
  0.0 61.9 %mix.1 = (f32[16,128]{1,0:T(8,128)S(1)}, s32[1,1]{1,0:T(1,128)}, s32[16,16,128]{2,1,0:T(8,128)S(1)}, f32[16,4,2,16,128]{4,3,2,1,0:T(8,128)S(1)}) custom-call(f32[16,16384]{1,0:T(8,128)} %panel_hbm.1, s32[128,128]{1,0:T(8,128)} %bitcast.10, s32[8,128]{1,0:T(8,128)} %bitcast.13, s32[8,128]{1,0:T(8,128)} %bitcast.14), custom_call_target="tpu_custom_call" | custom-call | tf_op jit(solution)/shard_map/mix/pallas_call | solution.py:487
  62.5 0.6 copy.11
  (1 shorter events, 0.0 us)

commit v6 on v5

--- a/solution.py
+++ b/solution.py
@@ -132,10 +132,14 @@
         return carry
 
     lax.fori_loop(0, 8, outer_high, 0)
-    pl.semaphore_wait(plane_sem, 3)
-    for d in range(1, 4):
-        tell(all_sem, at(z, x, (y + d) % 4, core))
-    pl.semaphore_wait(all_sem, 3)
+
+    def outer_low(g, carry):
+        vals = butterfly([y_ref[g * 8 + j] for j in range(8)])
+        for j in range(8):
+            y_ref[g * 8 + j] = vals[j]
+        return carry
+
+    lax.fori_loop(0, 16, outer_low, 0)
 
     slot = y * 32 + z * 4 + x
     to_x = [(x + d) % 4 for d in range(4)]
@@ -154,30 +158,29 @@
     def send_list(tz, dx):
         push(mine, lists.at[z % 4 * 4 + x], list_send, list_recv, at(tz, to_x[dx], y, core))
 
-    def first(i, carry):
-        tz = (z + i * 3 + 4) % 8
-        for g in range(2):
-            vals = butterfly([y_ref[tz * 16 + g * 8 + j] for j in range(8)])
-            for j in range(8):
-                y_ref[tz * 16 + g * 8 + j] = vals[j]
-        for dx in range(4):
-            if dx:
-                send(tz, dx, 0)
-                pl.when(sends_list)(functools.partial(send_list, tz, dx))
-            else:
-                pl.when(tz != z)(functools.partial(send, tz, 0, 0))
-                pl.when(sends_list & (tz != z))(functools.partial(send_list, tz, 0))
-        return carry
-
-    lax.fori_loop(0, 8, first, 0)
-
+    for d in (4, 7, 2, 5, 3, 6, 1):
+        tz = (z + d) % 8
+        send(tz, 0, 0)
+        pl.when(sends_list)(functools.partial(send_list, tz, 0))
+    pl.semaphore_wait(plane_sem, 3)
+    for d in range(1, 4):
+        tell(all_sem, at(z, x, (y + d) % 4, core))
+
+    def sweep(dy, carry_list):
+        def some(i, carry):
+            tz = (z + i * 3 + 4) % 8
+            for dx in range(1 if carry_list else 0, 4):
+                send(tz, dx, dy)
+                if carry_list:
+                    pl.when(sends_list)(functools.partial(send_list, tz, dx))
+            return carry
+
+        lax.fori_loop(0, 8, some, 0)
+
+    sweep(0, True)
+    pl.semaphore_wait(all_sem, 3)
     for dy in range(1, 4):
-        def later(i, carry):
-            for dx in range(4):
-                send((z + i * 3 + 4) % 8, dx, dy)
-            return carry
-
-        lax.fori_loop(0, 8, later, 0)
+        sweep(dy, False)
 
     r_ref[slot] = y_ref[z * 16 + x * 4 + y]
 
@@ -311,16 +314,16 @@
             sz[n, 8:16, :] = (b2[h, 0, i] + b2[h, 1, i]) + (b2[h, 2, i] + b2[h, 3, i])
             pl.when(z != n)(functools.partial(push, sz.at[n], zr.at[z], s3, r3, at(n, x, y, core)))
 
-    def step(j, carry):
-        pl.when(j < 4)(functools.partial(make, 2 * j))
-        pl.when((j >= 1) & (j < 5))(functools.partial(forward, 2 * j - 2))
-        pl.when(j < 4)(functools.partial(make, 2 * j + 1))
-        pl.when((j >= 1) & (j < 5))(functools.partial(forward, 2 * j - 1))
-        pl.when((j >= 2) & (j < 6))(functools.partial(second, j - 2))
-        pl.when(j >= 3)(functools.partial(third, j - 3))
-        return carry
-
-    lax.fori_loop(0, 7, step, 0)
+    def step(i, carry):
+        make(i)
+        forward(i - 1)
+        return carry
+
+    make(jnp.int32(0))
+    lax.fori_loop(1, 8, step, 0)
+    forward(jnp.int32(7))
+    for stage, h in ((second, 0), (second, 1), (third, 0), (second, 2), (third, 1), (second, 3), (third, 2), (third, 3)):
+        stage(h)
     zr[z] = sz[z]
     wait_bytes(zr.at[pl.ds(0, 7)], r3)
     v = [zr[i] for i in range(8)]

time: 63.2 us -> 58.9 us (0.932)
  the two profiles are of different devices: /device:TPU:2 before, /device:TPU:1 now
where the time goes in v6:
time: 58.9 us; the launch traced here: 58.8 us
  Pallas kernels  57.5 us (98%)
  between operations  0.65 us (1%)
  local copies, waits for them, and re-layouts  0.6 us (1%)
    pallas_call x1, Pallas kernels, body(): pl.pallas_call(mix_kernel, out_shape=[jax.ShapeDtypeStruct((16, 128), F32...  57.5 us

profile of v6, /device:TPU:1, one launch (start us, length us, event | category | flops | bytes accessed | tf_op | source)
XLA Modules:
  0.0 58.8 jit_solution(11691193809170217421)
XLA Ops:
  0.0 57.5 %mix.1 = (f32[16,128]{1,0:T(8,128)S(1)}, s32[1,1]{1,0:T(1,128)}, s32[16,16,128]{2,1,0:T(8,128)S(1)}, f32[16,4,2,16,128]{4,3,2,1,0:T(8,128)S(1)}) custom-call(f32[16,16384]{1,0:T(8,128)} %panel_hbm.1, s32[128,128]{1,0:T(8,128)} %bitcast.10, s32[8,128]{1,0:T(8,128)} %bitcast.13, s32[8,128]{1,0:T(8,128)} %bitcast.14), custom_call_target="tpu_custom_call" | custom-call | tf_op jit(solution)/shard_map/mix/pallas_call | solution.py:490
  58.2 0.6 %copy.11 = f32[1,16,128]{2,1,0:T(8,128)} copy(f32[1,16,128]{2,1,0:T(8,128)S(1)} %get-tuple-element.25) | data formatting | bytes 16384
  (1 shorter events, 0.0 us)

commit v7 on v6

--- a/solution.py
+++ b/solution.py
@@ -81,10 +81,10 @@
 
 def mix_kernel(
     panel_hbm, signs_hbm, offsets, owners, result, crowded, lists, kept_hbm,
-    panel, signs, y_ref, r_ref, t_ref, mine, out, lanes, ids, ranks, picks, names, picked, full_here, full_there,
-    g_ref, c_ref, ha, hb, a1, b1, sa, sb, a2, b2, sz, zr,
+    panel, signs, y_ref, r_ref, t_ref, mine, own, out, lanes, ids, ranks, picks, names_here, names_there,
+    s_here, s_there, picked, full_here, full_there, ha, hb, a1, b1, sa, sb, a2, b2, sz, zr,
     load_sem, small_sem, send_sem, recv_sem, core_send, core_recv, list_send, list_recv, plane_sem, all_sem,
-    keep_sem, full_send, full_recv, s0, r0, s1, r1a, r1b, s2, r2a, r2b, s3, r3,
+    keep_sem, full_send, full_recv, name_send, name_recv, pass_send, pass_recv, s0, r0, s1, r1a, r1b, s2, r2a, r2b, s3, r3,
 ):
     z, x, y, core = place()
     barrier = pltpu.get_barrier_semaphore()
@@ -96,8 +96,8 @@
 
     small = [
         pltpu.make_async_copy(signs_hbm, signs, small_sem.at[0]),
-        pltpu.make_async_copy(offsets, mine.at[pl.ds(0, 8)], small_sem.at[1]),
-        pltpu.make_async_copy(owners, mine.at[pl.ds(8, 8)], small_sem.at[2]),
+        pltpu.make_async_copy(offsets, own.at[pl.ds(0, 8)], small_sem.at[1]),
+        pltpu.make_async_copy(owners, own.at[pl.ds(8, 8)], small_sem.at[2]),
     ]
     small[0].start()
     for i in range(4):
@@ -148,6 +148,9 @@
 
     small[1].wait()
     small[2].wait()
+    for r in range(2):
+        mine[r : r + 1, :] = own[pl.ds(2 * y + r, 1), :]
+        mine[2 + r : 3 + r, :] = own[pl.ds(8 + 2 * y + r, 1), :]
 
     def send(tz, dx, dy):
         push(
@@ -156,7 +159,7 @@
         )
 
     def send_list(tz, dx):
-        push(mine, lists.at[z % 4 * 4 + x], list_send, list_recv, at(tz, to_x[dx], y, core))
+        push(mine, lists.at[y, z % 4 * 4 + x], list_send, list_recv, at(tz, to_x[dx], y, core))
 
     for d in (4, 7, 2, 5, 3, 6, 1):
         tz = (z + d) % 8
@@ -186,12 +189,16 @@
 
     @pl.when(sends_list)
     def _():
-        lists[z % 4 * 4 + x] = mine[...]
-        wait_bytes(lists.at[pl.ds(0, 15)], list_recv)
+        lists[y, z % 4 * 4 + x] = mine[...]
+        wait_bytes(lists.at[0, pl.ds(0, 15)], list_recv)
 
     @pl.when(jnp.logical_not(sends_list))
     def _():
-        wait_bytes(lists, list_recv)
+        wait_bytes(lists.at[0], list_recv)
+
+    for d in (2, 1, 3):
+        push(lists.at[y], lists.at[y], pass_send, pass_recv, at(z, x, to_y[d], core))
+    wait_bytes(lists.at[pl.ds(0, 3)], pass_recv)
 
     turn = (1 - 2 * core).astype(F32)
 
@@ -230,7 +237,8 @@
 
     nowhere = jnp.zeros((1, TAKEN), F32)
     spot, its_name = lax.fori_loop(0, 16, locate, (nowhere - 1.0, nowhere))
-    names[0:1, :] = its_name
+    names_here[...] = jnp.broadcast_to(its_name, (8, TAKEN))
+    push(names_here, names_there, name_send, name_recv, at(z, x, y, 1 - core))
 
     def mark(k, carry):
         rows = iota((256, TAKEN), 0).astype(F32) + (k * 256).astype(F32)
@@ -240,9 +248,10 @@
     lax.fori_loop(0, 8, mark, 0)
 
     def tally(p, count):
-        slabs = lists[p, 0:8, :] // 128
-        for b in range(8):
-            count = count + (slabs[b : b + 1, :] == iota((128, 128), 0)).astype(F32)
+        for q in range(4):
+            slabs = lists[q, p] // 128
+            for r in range(2):
+                count = count + (slabs[r : r + 1, :] == iota((128, 128), 0)).astype(F32)
         return count
 
     count = lax.fori_loop(0, 16, tally, jnp.zeros((128, 128), F32))
@@ -265,31 +274,35 @@
     for g in range(4):
         pick = picks[2 * g : 2 * g + 2].reshape(512, TAKEN)
         got = got + jnp.dot(stacked(out, g), pick, preferred_element_type=F32)
-    picked[...] = got.astype(BF16)
-
-    def make(i):
-        whole = picked[...]
+    s_here[...] = got[0:128] + got[128:256]
+    push(s_here, s_there, s0, r0, at(z, x, y, 1 - core))
+    picked[:, :, :, :, 0:TAKEN] = got.astype(BF16).reshape(2, 4, 2, 16, TAKEN)
+    wait_bytes(names_there, name_recv)
+    names = jnp.concatenate([names_here[0:1, :], names_there[0:1, :]], axis=1)
+    wait_bytes(s_there, r0)
+    hi, lo = split(s_there[...])
+    picked[0, :, :, :, TAKEN : 2 * TAKEN] = hi.reshape(4, 2, 16, TAKEN)
+    picked[1, :, :, :, TAKEN : 2 * TAKEN] = lo.reshape(4, 2, 16, TAKEN)
+
+    def make(i, carry):
+        whole = picked[...].reshape(256, 2 * TAKEN)
+        half = picked[:, :, core].reshape(128, 2 * TAKEN)
         members = []
         for tx in range(4):
             wanted = (i * 4 + tx + 1).astype(F32)
-            members.append(whole * (names[0:1, :] == wanted).astype(F32).astype(BF16))
-        members = jnp.concatenate(members, axis=0)
-        both = lax.dot_general(members, whole, NT, preferred_element_type=F32)
+            members.append(half * (names == wanted).astype(F32).astype(BF16))
+        both = lax.dot_general(jnp.concatenate(members, axis=0), whole, NT, preferred_element_type=F32)
         for tx in range(4):
-            g_ref[i, tx] = folded(both[256 * tx : 256 * tx + 256]).reshape(4, 2, 16, 128)
-        push(g_ref.at[i, :, :, 1 - core], c_ref.at[i], s0, r0.at[i], at(z, x, y, 1 - core))
-
-    def forward(i):
-        wait_bytes(c_ref.at[i], r0.at[i])
-        for tx in range(4):
-            for ty in range(4):
-                ha[i, tx, ty] = g_ref[i, tx, ty, core, 0:8, :] + c_ref[i, tx, ty, 0:8, :]
-                hb[i, ty, tx] = g_ref[i, tx, ty, core, 8:16, :] + c_ref[i, tx, ty, 8:16, :]
+            one = both[128 * tx : 128 * tx + 64] + both[128 * tx + 64 : 128 * tx + 128]
+            one = (one[:, :128] + one[:, 128:]).reshape(4, 2, 8, 128)
+            ha[i, tx] = one[:, 0]
+            hb[i, :, tx] = one[:, 1]
         for d in (2, 1, 3):
             push(ha.at[i, to_x[d]], a1.at[x, i], s1.at[0], r1a.at[i // 2], at(z, to_x[d], y, core))
             push(hb.at[i, to_y[d]], b1.at[y, i], s1.at[1], r1b.at[i // 2], at(z, x, to_y[d], core))
         a1[x, i] = ha[i, x]
         b1[y, i] = hb[i, y]
+        return carry
 
     def second(h):
         wait_bytes(a1.at[pl.ds(0, 3), pl.ds(0, 2)], r1a.at[h])
@@ -314,14 +327,7 @@
             sz[n, 8:16, :] = (b2[h, 0, i] + b2[h, 1, i]) + (b2[h, 2, i] + b2[h, 3, i])
             pl.when(z != n)(functools.partial(push, sz.at[n], zr.at[z], s3, r3, at(n, x, y, core)))
 
-    def step(i, carry):
-        make(i)
-        forward(i - 1)
-        return carry
-
-    make(jnp.int32(0))
-    lax.fori_loop(1, 8, step, 0)
-    forward(jnp.int32(7))
+    lax.fori_loop(0, 8, make, 0)
     for stage, h in ((second, 0), (second, 1), (third, 0), (second, 2), (third, 1), (second, 3), (third, 2), (third, 3)):
         stage(h)
     zr[z] = sz[z]
@@ -341,8 +347,10 @@
 
     keep.wait()
     wait_bytes(full_here, full_send)
+    wait_bytes(names_here, name_send)
+    wait_bytes(lists.at[pl.ds(0, 3)], pass_send)
+    wait_bytes(s_here, s0)
     wait_bytes(t_ref, core_send)
-    wait_bytes(c_ref, s0)
     wait_bytes(a1.at[pl.ds(0, 3)], s1.at[0])
     wait_bytes(b1.at[pl.ds(0, 3)], s1.at[1])
     wait_bytes(a2.at[:, pl.ds(0, 3)], s2.at[0])
@@ -351,8 +359,8 @@
 
 
 def ranked(lists, slab):
-    here = jnp.concatenate([lists[:, b, :] for b in range(8)], axis=1) - slab * 128
-    owner = jnp.concatenate([lists[:, 8 + b, :] for b in range(8)], axis=1)
+    here = jnp.concatenate([lists[b // 2, :, b % 2, :] for b in range(8)], axis=1) - slab * 128
+    owner = jnp.concatenate([lists[b // 2, :, 2 + b % 2, :] for b in range(8)], axis=1)
     inside = (here >= 0) & (here < 128)
     mask = jnp.where(inside, 1.0, 0.0).astype(F32)
     before = (iota((128, 128), 0) < iota((128, 128), 1)).astype(F32).astype(BF16)
@@ -492,7 +500,7 @@
         out_shape=[
             jax.ShapeDtypeStruct((16, 128), F32),
             jax.ShapeDtypeStruct((1, 1), jnp.int32),
-            jax.ShapeDtypeStruct((16, 16, 128), jnp.int32),
+            jax.ShapeDtypeStruct((4, 16, 4, 128), jnp.int32),
             jax.ShapeDtypeStruct((16, 4, 2, 16, 128), F32),
         ],
         in_specs=[HBM] * 4,
@@ -503,6 +511,7 @@
             vmem((128, 16, 128), F32),
             vmem((128, 16, 128), F32),
             vmem((4, 16, 16, 128), F32),
+            vmem((4, 128), jnp.int32),
             vmem((16, 128), jnp.int32),
             vmem((16, 4, 2, 16, 128), F32),
             vmem((16, 1024), F32),
@@ -510,11 +519,12 @@
             vmem((16, 1024), F32),
             vmem((8, 256, TAKEN), BF16),
             vmem((8, TAKEN), F32),
-            vmem((256, TAKEN), BF16),
+            vmem((8, TAKEN), F32),
+            vmem((128, TAKEN), F32),
+            vmem((128, TAKEN), F32),
+            vmem((2, 4, 2, 16, 2 * TAKEN), BF16),
             vmem((8, 128), jnp.int32),
             vmem((8, 128), jnp.int32),
-            vmem((8, 4, 4, 2, 16, 128), F32),
-            vmem((8, 4, 4, 16, 128), F32),
             vmem((8, 4, 4, 8, 128), F32),
             vmem((8, 4, 4, 8, 128), F32),
             vmem((4, 8, 4, 8, 128), F32),
@@ -527,7 +537,7 @@
             vmem((8, 16, 128), F32),
             dma((4,)), dma((3,)), dma, dma((4,)), dma, dma, dma, dma,
             pltpu.SemaphoreType.REGULAR, pltpu.SemaphoreType.REGULAR,
-            dma, dma, dma, dma, dma((8,)), dma((2,)), dma((4,)), dma((4,)),
+            dma, dma, dma, dma, dma, dma, dma, dma, dma, dma((2,)), dma((4,)), dma((4,)),
             dma((2,)), dma((4,)), dma((4,)), dma, dma,
         ],
         compiler_params=params(collective_id=1, vmem_limit_bytes=MIX_VMEM),

time: 58.9 us -> 56.4 us (0.958)
  the two profiles are of different devices: /device:TPU:1 before, /device:TPU:2 now
where the time goes in v7:
time: 56.4 us; the launch traced here: 55.8 us
  Pallas kernels  54.6 us (97%)
  between operations  0.65 us (1%)
  local copies, waits for them, and re-layouts  0.6 us (1%)
    pallas_call x1, Pallas kernels, body(): pl.pallas_call(mix_kernel, out_shape=[jax.ShapeDtypeStruct((16, 128), F32...  54.6 us

profile of v7, /device:TPU:2, one launch (start us, length us, event | category | flops | bytes accessed | tf_op | source)
XLA Modules:
  0.0 55.8 jit_solution(4095238845062200064)
XLA Ops:
  0.0 54.6 %mix.1 = (f32[16,128]{1,0:T(8,128)S(1)}, s32[1,1]{1,0:T(1,128)}, s32[4,16,4,128]{3,2,1,0:T(4,128)S(1)}, f32[16,4,2,16,128]{4,3,2,1,0:T(8,128)S(1)}) custom-call(f32[16,16384]{1,0:T(8,128)} %panel_hbm.1, s32[128,128]{1,0:T(8,128)} %bitcast.10, s32[8,128]{1,0:T(8,128)} %bitcast.13, s32[8,128]{1,0:T(8,128)} %bitcast.14), custom_call_target="tpu_custom_call" | custom-call | tf_op jit(solution)/shard_map/mix/pallas_call | solution.py:498
  55.2 0.6 %copy.11 = f32[1,16,128]{2,1,0:T(8,128)} copy(f32[1,16,128]{2,1,0:T(8,128)S(1)} %get-tuple-element.25) | data formatting | bytes 16384
  (1 shorter events, 0.0 us)

commit v8 on v7

--- a/solution.py
+++ b/solution.py
@@ -82,9 +82,9 @@
 def mix_kernel(
     panel_hbm, signs_hbm, offsets, owners, result, crowded, lists, kept_hbm,
     panel, signs, y_ref, r_ref, t_ref, mine, own, out, lanes, ids, ranks, picks, names_here, names_there,
-    s_here, s_there, picked, full_here, full_there, ha, hb, a1, b1, sa, sb, a2, b2, sz, zr,
+    s_here, s_there, picked, full_here, full_there, ha, hb, a1, b1, sa, sb, fa, fb,
     load_sem, small_sem, send_sem, recv_sem, core_send, core_recv, list_send, list_recv, plane_sem, all_sem,
-    keep_sem, full_send, full_recv, name_send, name_recv, pass_send, pass_recv, s0, r0, s1, r1a, r1b, s2, r2a, r2b, s3, r3,
+    keep_sem, full_send, full_recv, name_send, name_recv, pass_send, pass_recv, s0, r0, s1, r1a, r1b, s2, r2,
 ):
     z, x, y, core = place()
     barrier = pltpu.get_barrier_semaphore()
@@ -284,7 +284,8 @@
     picked[0, :, :, :, TAKEN : 2 * TAKEN] = hi.reshape(4, 2, 16, TAKEN)
     picked[1, :, :, :, TAKEN : 2 * TAKEN] = lo.reshape(4, 2, 16, TAKEN)
 
-    def make(i, carry):
+    def make(k, carry):
+        i = (z + k * 3 + 4) % 8
         whole = picked[...].reshape(256, 2 * TAKEN)
         half = picked[:, :, core].reshape(128, 2 * TAKEN)
         members = []
@@ -298,43 +299,42 @@
             ha[i, tx] = one[:, 0]
             hb[i, :, tx] = one[:, 1]
         for d in (2, 1, 3):
-            push(ha.at[i, to_x[d]], a1.at[x, i], s1.at[0], r1a.at[i // 2], at(z, to_x[d], y, core))
-            push(hb.at[i, to_y[d]], b1.at[y, i], s1.at[1], r1b.at[i // 2], at(z, x, to_y[d], core))
+            push(ha.at[i, to_x[d]], a1.at[x, i], s1.at[0], r1a.at[i], at(z, to_x[d], y, core))
+            push(hb.at[i, to_y[d]], b1.at[y, i], s1.at[1], r1b.at[i], at(z, x, to_y[d], core))
         a1[x, i] = ha[i, x]
         b1[y, i] = hb[i, y]
         return carry
 
-    def second(h):
-        wait_bytes(a1.at[pl.ds(0, 3), pl.ds(0, 2)], r1a.at[h])
-        wait_bytes(b1.at[pl.ds(0, 3), pl.ds(0, 2)], r1b.at[h])
-        for i in range(2):
-            for t in range(4):
-                n = 2 * h + i
-                sa[h, t, i] = (a1[0, n, t] + a1[1, n, t]) + (a1[2, n, t] + a1[3, n, t])
-                sb[h, t, i] = (b1[0, n, t] + b1[1, n, t]) + (b1[2, n, t] + b1[3, n, t])
-        for d in (2, 1, 3):
-            push(sa.at[h, to_y[d]], a2.at[h, y], s2.at[0], r2a.at[h], at(z, x, to_y[d], core))
-            push(sb.at[h, to_x[d]], b2.at[h, x], s2.at[1], r2b.at[h], at(z, to_x[d], y, core))
-        a2[h, y] = sa[h, y]
-        b2[h, x] = sb[h, x]
-
-    def third(h):
-        wait_bytes(a2.at[h, pl.ds(0, 3)], r2a.at[h])
-        wait_bytes(b2.at[h, pl.ds(0, 3)], r2b.at[h])
-        for i in range(2):
-            n = 2 * h + i
-            sz[n, 0:8, :] = (a2[h, 0, i] + a2[h, 1, i]) + (a2[h, 2, i] + a2[h, 3, i])
-            sz[n, 8:16, :] = (b2[h, 0, i] + b2[h, 1, i]) + (b2[h, 2, i] + b2[h, 3, i])
-            pl.when(z != n)(functools.partial(push, sz.at[n], zr.at[z], s3, r3, at(n, x, y, core)))
+    def direct(k, carry):
+        i = (z + k * 3 + 4) % 8
+        wait_bytes(a1.at[pl.ds(0, 3), i], r1a.at[i])
+        for t in range(4):
+            sa[i, t] = (a1[0, i, t] + a1[1, i, t]) + (a1[2, i, t] + a1[3, i, t])
+        for d in (2, 1, 3, 0):
+            go = functools.partial(
+                push, sa.at[i, to_y[d]], fa.at[z * 4 + y], s2.at[0], r2.at[0], at(i, x, to_y[d], core)
+            )
+            go() if d else pl.when(i != z)(go)
+        wait_bytes(b1.at[pl.ds(0, 3), i], r1b.at[i])
+        for t in range(4):
+            sb[i, t] = (b1[0, i, t] + b1[1, i, t]) + (b1[2, i, t] + b1[3, i, t])
+        for d in (2, 1, 3, 0):
+            go = functools.partial(
+                push, sb.at[i, to_x[d]], fb.at[z * 4 + x], s2.at[1], r2.at[1], at(i, to_x[d], y, core)
+            )
+            go() if d else pl.when(i != z)(go)
+        return carry
 
     lax.fori_loop(0, 8, make, 0)
-    for stage, h in ((second, 0), (second, 1), (third, 0), (second, 2), (third, 1), (second, 3), (third, 2), (third, 3)):
-        stage(h)
-    zr[z] = sz[z]
-    wait_bytes(zr.at[pl.ds(0, 7)], r3)
-    v = [zr[i] for i in range(8)]
-    total = ((v[0] + v[1]) + (v[2] + v[3])) + ((v[4] + v[5]) + (v[6] + v[7]))
-    result[...] = total * GRAM_SCALE
+    lax.fori_loop(0, 8, direct, 0)
+    fa[z * 4 + y] = sa[z, y]
+    fb[z * 4 + x] = sb[z, x]
+    for n, ref in enumerate((fa, fb)):
+        wait_bytes(ref.at[pl.ds(0, 31)], r2.at[n])
+        parts = [ref[i] for i in range(32)]
+        while len(parts) > 1:
+            parts = [a + b for a, b in zip(parts[::2], parts[1::2])]
+        result[8 * n : 8 * n + 8, :] = parts[0] * GRAM_SCALE
     wait_bytes(full_there, full_recv)
     crowded[0, 0] = jnp.max(jnp.maximum(full_here[...], full_there[...]))
 
@@ -353,9 +353,8 @@
     wait_bytes(t_ref, core_send)
     wait_bytes(a1.at[pl.ds(0, 3)], s1.at[0])
     wait_bytes(b1.at[pl.ds(0, 3)], s1.at[1])
-    wait_bytes(a2.at[:, pl.ds(0, 3)], s2.at[0])
-    wait_bytes(b2.at[:, pl.ds(0, 3)], s2.at[1])
-    wait_bytes(zr.at[pl.ds(0, 7)], s3)
+    wait_bytes(fa.at[pl.ds(0, 31)], s2.at[0])
+    wait_bytes(fb.at[pl.ds(0, 31)], s2.at[1])
 
 
 def ranked(lists, slab):
@@ -529,16 +528,14 @@
             vmem((8, 4, 4, 8, 128), F32),
             vmem((4, 8, 4, 8, 128), F32),
             vmem((4, 8, 4, 8, 128), F32),
-            vmem((4, 4, 2, 8, 128), F32),
-            vmem((4, 4, 2, 8, 128), F32),
-            vmem((4, 4, 2, 8, 128), F32),
-            vmem((4, 4, 2, 8, 128), F32),
-            vmem((8, 16, 128), F32),
-            vmem((8, 16, 128), F32),
+            vmem((8, 4, 8, 128), F32),
+            vmem((8, 4, 8, 128), F32),
+            vmem((32, 8, 128), F32),
+            vmem((32, 8, 128), F32),
             dma((4,)), dma((3,)), dma, dma((4,)), dma, dma, dma, dma,
             pltpu.SemaphoreType.REGULAR, pltpu.SemaphoreType.REGULAR,
-            dma, dma, dma, dma, dma, dma, dma, dma, dma, dma((2,)), dma((4,)), dma((4,)),
-            dma((2,)), dma((4,)), dma((4,)), dma, dma,
+            dma, dma, dma, dma, dma, dma, dma, dma, dma, dma((2,)), dma((8,)), dma((8,)),
+            dma((2,)), dma((2,)),
         ],
         compiler_params=params(collective_id=1, vmem_limit_bytes=MIX_VMEM),
         name="mix",

time: 56.4 us -> 54.9 us (0.973)
  Pallas kernels: 54.6 us -> 53.5 us
    pallas_call x1, Pallas kernels: 54.6 us -> 53.5 us  [body(): pl.pallas_call(mix_kernel, out_shape=[jax.ShapeDtypeStruct((16, 128), F32...]
where the time goes in v8:
time: 54.9 us; the launch traced here: 54.8 us
  Pallas kernels  53.5 us (97%)
  between operations  0.65 us (1%)
  local copies, waits for them, and re-layouts  0.6 us (1%)
    pallas_call x1, Pallas kernels, body(): pl.pallas_call(mix_kernel, out_shape=[jax.ShapeDtypeStruct((16, 128), F32...  53.5 us

profile of v8, /device:TPU:2, one launch (start us, length us, event | category | flops | bytes accessed | tf_op | source)
XLA Modules:
  0.0 54.8 jit_solution(15561691475559684670)
XLA Ops:
  0.0 53.5 %mix.1 = (f32[16,128]{1,0:T(8,128)S(1)}, s32[1,1]{1,0:T(1,128)}, s32[4,16,4,128]{3,2,1,0:T(4,128)S(1)}, f32[16,4,2,16,128]{4,3,2,1,0:T(8,128)S(1)}) custom-call(f32[16,16384]{1,0:T(8,128)} %panel_hbm.1, s32[128,128]{1,0:T(8,128)} %bitcast.10, s32[8,128]{1,0:T(8,128)} %bitcast.13, s32[8,128]{1,0:T(8,128)} %bitcast.14), custom_call_target="tpu_custom_call" | custom-call | tf_op jit(solution)/shard_map/mix/pallas_call | solution.py:497
  54.2 0.6 %copy.11 = f32[1,16,128]{2,1,0:T(8,128)} copy(f32[1,16,128]{2,1,0:T(8,128)S(1)} %get-tuple-element.25) | data formatting | bytes 16384
  (1 shorter events, 0.0 us)

commit v9 on v8

--- a/solution.py
+++ b/solution.py
@@ -285,7 +285,7 @@
     picked[1, :, :, :, TAKEN : 2 * TAKEN] = lo.reshape(4, 2, 16, TAKEN)
 
     def make(k, carry):
-        i = (z + k * 3 + 4) % 8
+        i = (z + 4 + k // 2 * (1 - k % 2) - (k + 1) // 2 * (k % 2)) % 8
         whole = picked[...].reshape(256, 2 * TAKEN)
         half = picked[:, :, core].reshape(128, 2 * TAKEN)
         members = []
@@ -306,7 +306,7 @@
         return carry
 
     def direct(k, carry):
-        i = (z + k * 3 + 4) % 8
+        i = (z + 4 + k // 2 * (1 - k % 2) - (k + 1) // 2 * (k % 2)) % 8
         wait_bytes(a1.at[pl.ds(0, 3), i], r1a.at[i])
         for t in range(4):
             sa[i, t] = (a1[0, i, t] + a1[1, i, t]) + (a1[2, i, t] + a1[3, i, t])

time: 54.9 us -> 54.1 us (0.985)
  Pallas kernels: 53.5 us -> 52.7 us
    pallas_call x1, Pallas kernels: 53.5 us -> 52.7 us  [body(): pl.pallas_call(mix_kernel, out_shape=[jax.ShapeDtypeStruct((16, 128), F32...]
where the time goes in v9:
time: 54.1 us; the launch traced here: 54 us
  Pallas kernels  52.7 us (97%)
  between operations  0.65 us (1%)
  local copies, waits for them, and re-layouts  0.6 us (1%)
    pallas_call x1, Pallas kernels, body(): pl.pallas_call(mix_kernel, out_shape=[jax.ShapeDtypeStruct((16, 128), F32...  52.7 us

profile of v9, /device:TPU:2, one launch (start us, length us, event | category | flops | bytes accessed | tf_op | source)
XLA Modules:
  0.0 54.0 jit_solution(12487202469645042462)
XLA Ops:
  0.0 52.7 %mix.1 = (f32[16,128]{1,0:T(8,128)S(1)}, s32[1,1]{1,0:T(1,128)}, s32[4,16,4,128]{3,2,1,0:T(4,128)S(1)}, f32[16,4,2,16,128]{4,3,2,1,0:T(8,128)S(1)}) custom-call(f32[16,16384]{1,0:T(8,128)} %panel_hbm.1, s32[128,128]{1,0:T(8,128)} %bitcast.10, s32[8,128]{1,0:T(8,128)} %bitcast.13, s32[8,128]{1,0:T(8,128)} %bitcast.14), custom_call_target="tpu_custom_call" | custom-call | tf_op jit(solution)/shard_map/mix/pallas_call | solution.py:497
  53.4 0.6 %copy.11 = f32[1,16,128]{2,1,0:T(8,128)} copy(f32[1,16,128]{2,1,0:T(8,128)S(1)} %get-tuple-element.25) | data formatting | bytes 16384
  (1 shorter events, 0.0 us)
